TPU v7x, 256 devices: a whole 4x4x8 slice. The times are simulated.
256 devices in a mesh: dp: 128 (over y_hi, z, x, core), mp: 2 (over y_lo).
Axes of the slice: x: 4, y: 4 (y_hi: 2, y_lo: 2; y = y_hi * 2 + y_lo), z: 8, core: 2. Of those that a mesh axis runs over, the one named last changes fastest.
Arguments:
- query_hidden: bfloat16 [1024, 4096], P('dp', 'mp'), may hold values from -0.119628906 to 0.119628906
- passage_hidden: bfloat16 [1024, 4096], P('dp', 'mp'), may hold values from -0.119628906 to 0.119628906
- hard_hidden: bfloat16 [65536, 4096], P('dp', 'mp'), may hold values from -0.119628906 to 0.119628906
- gain: float32 [4096], P('mp'), may hold values from 0.5 to 1.5
- hard_owner: int32 [1024, 31, 1], P('dp'), may hold values from 0 to 127; in each aligned block of 248 rows (0 to 247, 248 to 495, ..., all dimensions but the last counted through in order) at most 3 rows name the same one
- hard_slot: int32 [1024, 31], P('dp'), may hold values from 0 to 511
Outputs:
- grad_query_hidden: bfloat16 [1024, 4096], P('dp', 'mp')
- grad_passage_hidden: bfloat16 [1024, 4096], P('dp', 'mp')
- grad_hard_hidden: bfloat16 [65536, 4096], P('dp', 'mp')
- grad_gain: float32 [4096], P('mp')
- loss: float32 [], replicated
Inputs may be any that keep to these rules, and one draw needn't show every extreme that they name: `hard_owner`: among the 248 hard negatives of the queries of one index of dp, no owner is named more than 3 times, a bound that some block reaches.
All inputs are finite; a program needn't handle non-finite values.
Results may differ from a plain program's by a relative error of at most 0.01105.
Values may be sent and summed in bfloat16 or wider, within the bound.
No kernel may reach another device: no remote copies, remote signals or barrier semaphores. Data moves between devices by JAX's collectives and lax.ppermute only.
A program may use at most 64 MiB of HBM per device.

v0:
```python
import functools

import jax
import jax.numpy as jnp
from jax import lax
from jax.experimental import pallas as pl
from jax.experimental.pallas import tpu as pltpu
from jax.sharding import PartitionSpec as P

D = 4096
normalizer_divisor = 0.02
eps_norm = 1e-06
f32 = jnp.float32
bf16 = jnp.bfloat16
C, X, Z, YH = 1, (2, 4), (8, 16, 32), 64
SWAP = [(0, 1), (1, 0)]


def flip(x, mask):
    return lax.ppermute(x, "dp", [(i, i ^ mask) for i in range(128)])


def double(x, mask):
    return jnp.concatenate([x, flip(x, mask)], 0)


STEPS = ((Z[0], 64), (Z[1], 32), (Z[2], 16), (YH, 8))


def stats(values, gain):
    squares = values * values
    return jnp.sum(squares, axis=1), jnp.sum(squares * gain * gain, axis=1)


def scales(total_sq, total_gsq):
    scale = lax.rsqrt(total_sq / D + eps_norm)
    length = jnp.sqrt(scale * scale * total_gsq + eps_norm)
    return scale, length


def back_rows(values, gain, scale, length, grad_unit, dot):
    ratio = (scale / length)[:, None]
    return (
        ratio * gain * (grad_unit - values * ratio * gain * dot[:, None])
        - values * (scale * scale * dot * eps_norm / (length * length * D))[:, None]
    ).astype(bf16)


def tie(*arrays):
    return lax.optimization_barrier(arrays)


def requests(hard_owner, hard_slot):
    owner = hard_owner.reshape(-1)
    slot = hard_slot.reshape(-1)
    number = jnp.arange(owner.shape[0], dtype=jnp.int32)
    earlier = (owner[:, None] == owner[None, :]) & (number[:, None] < number[None, :])
    position = jnp.sum(earlier.astype(jnp.int32), axis=0)
    low = slot % 256
    high = 1 + slot // 256 + 2 * (number // hard_slot.shape[1])
    place = jnp.arange(8, dtype=jnp.int32)[:, None]
    coded = jnp.where(
        place // 2 == position[None, :], jnp.where(place % 2 == 0, low[None, :], high[None, :]), 0
    ).astype(bf16)
    names = (owner[:, None] == jnp.arange(128, dtype=jnp.int32)[None, :]).astype(bf16)
    return jnp.dot(coded, names, preferred_element_type=f32).astype(bf16)


def diagonal(rows):
    shape = (rows, 128)
    return lax.broadcasted_iota(jnp.int32, shape, 0) == lax.broadcasted_iota(jnp.int32, shape, 1)


def as_row(column):
    return jnp.sum(jnp.where(diagonal(column.shape[0]), column, 0.0), axis=0, keepdims=True)


def as_column(row, rows):
    return jnp.sum(jnp.where(diagonal(rows), row, 0.0), axis=1, keepdims=True)


def score_kernel(panel, passages, gain, *refs):
    pair_q, near, out = refs[:4], refs[4:8], refs[8]
    g = gain[...]
    rows = panel[:, :2048]
    scaled = passages[...].astype(f32) * g
    high = scaled.astype(bf16)
    low = (scaled - high.astype(f32)).astype(bf16)
    contract = (((1,), (1,)), ((), ()))
    out[0:64] = lax.dot_general(
        high, rows, contract, preferred_element_type=f32
    ) + lax.dot_general(low, rows, contract, preferred_element_type=f32)
    values = rows.astype(f32)
    squares = values * values
    out[64:65] = as_row(jnp.sum(squares, axis=1, keepdims=True))
    out[65:66] = as_row(jnp.sum(squares * (g * g), axis=1, keepdims=True))
    for s in range(4):
        product = pair_q[s][...].astype(f32) * near[s][...].astype(f32) * g
        out[66 + s : 67 + s] = as_row(jnp.sum(product, axis=1, keepdims=True))
    out[70:72] = jnp.zeros((2, 128), f32)


def route_kernel(me_ref, asked, panel, table_a, table_b, *refs):
    near, pair_q, query, slots = refs[:4], refs[4:8], refs[8], refs[9]
    me = me_ref[0]
    row = lax.broadcasted_iota(jnp.int32, (96, 128), 0)
    entry = row >> 4
    entry = jnp.where(entry >= 3, 2 * entry - 5, 2 * entry)
    pick = (lax.broadcasted_iota(jnp.int32, (96, 128), 1) == (row & 15) * 8 + entry).astype(bf16)
    lane = lax.broadcasted_iota(jnp.int32, (96, 128), 1)
    block = lax.broadcasted_iota(jnp.int32, (48, 1), 0) & 15

    def decode(entries, column):
        values = jnp.sum(jnp.where(lane == column, entries, 0.0), axis=1, keepdims=True)
        low, high = values[:48].astype(jnp.int32), values[48:].astype(jnp.int32)
        slot = jnp.where(high > 0, low + 256 * ((high - 1) & 1), -1)
        return slot, jnp.where(high > 0, block * 8 + ((high - 1) >> 1), -1)

    def row_of(index):
        return as_row((index + 1).astype(f32)).astype(jnp.int32) - 1

    def one_hot(index, count):
        lanes = lax.broadcasted_iota(jnp.int32, (index.shape[0], count), 1)
        return (lanes == index).astype(f32)

    picks = ([], [])
    for s in range(4):
        entries = jnp.dot(pick, asked[s], preferred_element_type=f32)
        for t in range(2):
            slot, _ = decode(entries, me ^ t)
            picks[t].append(one_hot(slot, 512))
            slots[4 * t + s : 4 * t + s + 1] = row_of(slot)
        if s == 0:
            mine = entries
    rows = [
        jnp.dot(
            jnp.concatenate(picks[t], 0).astype(bf16), table[...], preferred_element_type=f32
        ).astype(bf16)
        for t, table in enumerate((table_a, table_b))
    ]
    for s in range(4):
        for t in range(2):
            near[s][48 * t : 48 * t + 48] = rows[t][48 * s : 48 * s + 48]
        index = jnp.concatenate([decode(mine, me ^ (2 * s + t))[1] for t in range(2)], 0)
        query[s : s + 1] = row_of(index)
        pair_q[s][...] = jnp.dot(
            one_hot(index, 128).astype(bf16), panel[:, :2048], preferred_element_type=f32
        ).astype(bf16)
    query[4:8] = jnp.full((4, 128), -1, jnp.int32)


def put_sums(message, rows, v):
    high = v.astype(bf16).astype(f32)
    middle = (v - high).astype(bf16).astype(f32)
    parts = [high, middle, v - high - middle, jnp.zeros((10, 128), f32)]
    message[rows : rows + 16, :128] = jnp.concatenate(parts, 0).astype(bf16)
    message[rows : rows + 16, 128:] = jnp.zeros((16, 1920), bf16)


def swap_lanes(v, bit):
    v = jnp.concatenate([v, jnp.zeros((6, 128), f32)], 0)
    lane = lax.broadcasted_iota(jnp.int32, (8, 128), 1)
    swapped = jnp.where(
        (lane & bit) > 0, pltpu.roll(v, bit, axis=1), pltpu.roll(v, 128 - bit, axis=1)
    )
    return swapped[:2]


def halve_kernel(bit, kept, got, sums, *refs):
    rows = kept.shape[0]
    total = kept[...].astype(f32) + got[:rows].astype(f32)
    if rows > 8:
        add = got[rows : rows + 16, :128].astype(f32)
        add = add[:2] + add[2:4] + add[4:6]
    else:
        add = got[8:10, :128]
    v = sums[0:2] + swap_lanes(add, bit)
    refs[0][0:2] = v
    refs[0][2:8] = jnp.zeros((6, 128), f32)
    half = rows // 2
    refs[1][...] = total[:half].astype(refs[1].dtype) if rows > 8 else total
    if rows > 16:
        refs[2][:half] = total[half:].astype(bf16)
        put_sums(refs[2], half, v)
    elif rows > 8:
        refs[2][0:8] = total[8:]
        refs[2][8:16, :128] = jnp.concatenate([v, jnp.zeros((6, 128), f32)], 0)
        refs[2][8:16, 128:] = jnp.zeros((8, 1920), f32)


def halve(kept, message, sums, mask, bit):
    rows = kept.shape[0]
    shapes = [jax.ShapeDtypeStruct((8, 128), f32)]
    if rows > 16:
        shapes.append(jax.ShapeDtypeStruct((rows // 2, 2048), bf16))
        shapes.append(jax.ShapeDtypeStruct((rows // 2 + 16, 2048), bf16))
    elif rows > 8:
        shapes.append(jax.ShapeDtypeStruct((8, 2048), f32))
        shapes.append(jax.ShapeDtypeStruct((16, 2048), f32))
    else:
        shapes.append(jax.ShapeDtypeStruct((8, 2048), f32))
    sums, kept, *message = call(functools.partial(halve_kernel, bit), *shapes)(
        kept, flip(message, mask), sums
    )
    return kept, message[0] if message else None, sums


def pull_kernel(part, got, query, passages, *refs):
    near, kept, message, sums, small = refs[:4], refs[4], refs[5], refs[6], refs[7]
    full = part[...] + got[...]
    scale = lax.rsqrt(full[64:65] / D + eps_norm)
    length = jnp.sqrt(scale * scale * full[65:66] + eps_norm)
    ratio = scale / length
    ratio_column = as_column(ratio, 128)
    s_in = full[:64] * ratio / normalizer_divisor
    e_in = jnp.exp(s_in)
    own = diagonal(64) & (lax.broadcasted_iota(jnp.int32, (64, 128), 0) < 8)
    total = lax.dot_general(
        jnp.where(own, 0.0, e_in).astype(bf16),
        passages[...],
        (((0,), (0,)), ((), ())),
        preferred_element_type=f32,
    )
    z = jnp.zeros((128, 1), f32)
    w = jnp.zeros((128, 1), f32)
    for s in range(4):
        asker = query[s : s + 1, :]
        pick = lax.broadcasted_iota(jnp.int32, (128, 128), 0) == asker
        ratio_pair = jnp.sum(jnp.where(pick, ratio_column, 0.0), axis=0, keepdims=True)
        s_pair = full[66 + s : 67 + s] * ratio_pair / normalizer_divisor
        e_pair = jnp.where(asker >= 0, jnp.exp(s_pair), 0.0)
        spread = jnp.where(pick, e_pair, 0.0)
        z = z + jnp.sum(spread, axis=1, keepdims=True)
        w = w + jnp.sum(spread * s_pair, axis=1, keepdims=True)
        total = total + jnp.dot(
            spread[:, :96].astype(bf16), near[s][...], preferred_element_type=f32
        )
        small[66 + s : 67 + s] = s_pair
        small[70 + s : 71 + s] = e_pair
        small[74 + s : 75 + s] = ratio_pair
    kept[...] = total[:64].astype(bf16)
    message[0:64] = total[64:].astype(bf16)
    small[0:64] = s_in
    z = jnp.sum(e_in, axis=0, keepdims=True) + as_row(z)
    w = jnp.sum(e_in * s_in, axis=0, keepdims=True) + as_row(w)
    v = jnp.concatenate([z, w], 0)
    put_sums(message, 64, v)
    sums[0:2] = v
    sums[2:8] = jnp.zeros((6, 128), f32)
    small[64:66] = v
    small[78:79] = scale
    small[79:80] = length


def weigh_kernel(sums, small, query, panel, passages, gain, own_ref, *refs):
    pair_q, near, packed, late = refs[:4], refs[4:8], refs[8], refs[9:13]
    g = gain[...]
    z, w = sums[0:1], sums[1:2]
    s_in = small[0:64]
    scale, length = small[78:79], small[79:80]
    ratio = scale / length
    own = diagonal(64) & (lax.broadcasted_iota(jnp.int32, (64, 128), 0) < 8)
    c_in = ((jnp.exp(s_in) / z - jnp.where(own, 1.0, 0.0)) * ratio).astype(bf16)
    grads = jnp.dot(c_in, panel[:, :2048], preferred_element_type=f32)
    dots = jnp.sum(c_in.astype(f32) * (s_in / ratio), axis=1, keepdims=True)
    z_column = as_column(z, 128)
    values = passages[...].astype(f32)
    first = jnp.sum(grads * values, axis=0, keepdims=True)
    second = jnp.sum(values * values * dots, axis=0, keepdims=True)
    for s in range(4):
        asker = query[s : s + 1, :]
        pick = lax.broadcasted_iota(jnp.int32, (128, 128), 0) == asker
        z_pair = jnp.sum(jnp.where(pick, z_column, 0.0), axis=0, keepdims=True)
        c_pair = jnp.where(asker >= 0, small[70 + s : 71 + s] / z_pair, 0.0)
        ratio_pair = small[74 + s : 75 + s]
        coeff = (c_pair * ratio_pair).astype(bf16).astype(f32)
        pair_dot = jnp.where(asker >= 0, coeff * small[66 + s : 67 + s] / ratio_pair, 0.0)
        h = near[s][...].astype(f32)
        first = first + jnp.sum(
            pair_q[s][...].astype(f32) * h * as_column(coeff, 96), axis=0, keepdims=True
        )
        second = second + jnp.sum(h * h * as_column(pair_dot, 96), axis=0, keepdims=True)
        late[s][0:8, :2048] = grads[8 * s : 8 * s + 8]
        late[s][8:16, :2048] = grads[8 * s + 32 : 8 * s + 40]
        late[s][0:1, 2048:] = coeff
        late[s][1:2, 2048:] = pair_dot
        late[s][2:3, 2048:] = as_row(
            jnp.concatenate([dots[8 * s : 8 * s + 8], dots[8 * s + 32 : 8 * s + 40]], 0)
        )
        late[s][3:16, 2048:] = jnp.zeros((13, 128), f32)
    s_own = jnp.sum(jnp.where(own, s_in, 0.0), axis=0, keepdims=True)
    dot_own = as_column(w / z - s_own, 8)
    ratio_own = as_column(ratio, 8)
    direct = own_ref[...].astype(f32) * ratio_own
    third = jnp.sum(direct * direct * g * dot_own, axis=0, keepdims=True)
    result = first * (2.0 / normalizer_divisor) - second / g - third
    for i in range(16):
        packed[i : i + 1] = result[:, 128 * i : 128 * i + 128]
    lane = lax.broadcasted_iota(jnp.int32, (1, 128), 1)
    loss = jnp.sum(jnp.where(lane < 8, jnp.log(z) - s_own, 0.0), axis=1, keepdims=True)
    packed[16:24] = jnp.broadcast_to(loss, (8, 128))


def call(kernel, *shapes):
    return pl.pallas_call(
        kernel,
        out_shape=shapes,
        compiler_params=pltpu.CompilerParams(vmem_limit_bytes=40 * 1024 * 1024),
    )


def local(query_hidden, passage_hidden, hard_hidden, gain, hard_owner, hard_slot):
    me = lax.axis_index("dp")
    p_vals = passage_hidden.astype(f32)
    h_vals = hard_hidden.astype(f32)
    p_sq, p_gsq = stats(p_vals, gain)
    h_sq, h_gsq = stats(h_vals, gain)
    mine = jnp.concatenate([p_sq, p_gsq, h_sq, h_gsq])
    table = requests(hard_owner, hard_slot)
    panel = double(jnp.concatenate([query_hidden, table], 1), YH)
    panel, mine = tie(panel, mine)
    panel = double(panel, Z[2])
    tot = mine + lax.ppermute(mine, "mp", SWAP)
    panel, tot = tie(panel, tot)
    panel = double(panel, Z[1])
    p_scale, p_length = scales(tot[:8], tot[8:16])
    h_scale, h_length = scales(tot[16:528], tot[528:])
    p_emb = (p_vals * (p_scale / p_length)[:, None] * gain).astype(bf16)
    h_emb = (h_vals * (h_scale / h_length)[:, None] * gain).astype(bf16)
    panel, p_emb, h_emb = tie(panel, p_emb, h_emb)
    panel = double(panel, Z[0])
    p_all = jnp.concatenate([p_emb] + [flip(p_emb, 2 * s) for s in (1, 2, 3)], 0)
    h_other = flip(h_emb, C)
    panel, p_all, h_other = tie(panel, p_all, h_other)
    asked = panel[:, 2048:]
    asked = jnp.stack([asked] + [flip(asked, 2 * s) for s in (1, 2, 3)])
    p_all = jnp.concatenate([p_all, flip(p_all, C)], 0)

    wide = jax.ShapeDtypeStruct((96, 2048), bf16)
    index = jax.ShapeDtypeStruct((8, 128), jnp.int32)
    *both, query, slots = pl.pallas_call(
        route_kernel,
        out_shape=[wide] * 8 + [index] * 2,
        in_specs=[pl.BlockSpec(memory_space=pltpu.SMEM)] + [pl.BlockSpec(memory_space=pltpu.VMEM)] * 4,
        compiler_params=pltpu.CompilerParams(vmem_limit_bytes=40 * 1024 * 1024),
    )(me[None], asked, panel, h_emb, h_other)
    near, pair_q = both[:4], both[4:]
    near = [near[0]] + [flip(near[s], 2 * s) for s in (1, 2, 3)]
    gain_row = gain[None]

    (part,) = call(score_kernel, jax.ShapeDtypeStruct((72, 128), f32))(
        panel, p_all, gain_row, *pair_q, *near
    )
    got = lax.ppermute(part, "mp", SWAP)
    kept, message, sums, small = call(
        pull_kernel,
        jax.ShapeDtypeStruct((64, 2048), bf16),
        jax.ShapeDtypeStruct((80, 2048), bf16),
        jax.ShapeDtypeStruct((8, 128), f32),
        jax.ShapeDtypeStruct((80, 128), f32),
    )(part, got, query, p_all, *near)
    back = [pair_q[0]] + [flip(pair_q[s], 2 * s) for s in (1, 2, 3)]
    for mask, bit in STEPS:
        kept, message, sums = halve(kept, message, sums, mask, bit)
    pulled, sums, *back = tie(kept, sums, *back)
    packed, *late = call(
        weigh_kernel,
        jax.ShapeDtypeStruct((24, 128), f32),
        *[jax.ShapeDtypeStruct((16, 2176), f32)] * 4,
    )(sums, small, query, panel, p_all, gain_row, query_hidden, *pair_q, *near)
    packed = packed + flip(packed, C)
    packed, *late = tie(packed, *late)
    pair_q_other = flip(jnp.concatenate([block[48:] for block in back], 0), C)
    slot_other = flip(slots[4:], C)
    z_own, w_own = sums[0, :8], sums[1, :8]
    s_own = jnp.sum(jnp.where(jnp.eye(8, dtype=bool), small[:8, :8], 0.0), axis=1)
    e_own = jnp.exp(s_own)
    dot_q = w_own / z_own - s_own
    q_vals = query_hidden.astype(f32)
    q_scale, q_length = small[78, :8], small[79, :8]
    late = [late[0]] + [flip(late[s], 2 * s) for s in (1, 2, 3)]
    for mask in X:
        packed = packed + flip(packed, mask)
    packed, *late = tie(packed, *late)

    ge_p = sum(block[:, :2048] for block in late)
    dot_p = sum(block[2, 2048:2064] for block in late)
    coeff = jnp.concatenate([block[0, 2048:2144] for block in late]).reshape(4, 2, 48)
    pair_dot = jnp.concatenate([block[1, 2048:2144] for block in late]).reshape(4, 2, 48)
    give = jnp.concatenate(
        [
            ge_p[8:],
            jnp.concatenate(
                [
                    jnp.pad(coeff[:, 1].reshape(1, 192), ((0, 0), (0, 64))),
                    jnp.pad(pair_dot[:, 1].reshape(1, 192), ((0, 0), (0, 64))),
                    jnp.pad(dot_p[None, 8:], ((0, 0), (0, 248))),
                    jnp.zeros((5, 256), f32),
                ],
                0,
            ),
        ],
        1,
    )
    got = flip(give, C)
    packed = packed + flip(packed, Z[0])
    packed, got = tie(packed, got)
    for mask in (Z[1], Z[2], YH):
        packed = packed + flip(packed, mask)
    ge_p = (ge_p[:8] + got[:, :2048]) * gain / normalizer_divisor
    dot_p = dot_p[:8] + got[2, 2048:2056]
    coeff = jnp.concatenate([coeff[:, 0].reshape(-1), got[0, 2048:2240]])
    pair_dot = jnp.concatenate([pair_dot[:, 0].reshape(-1), got[1, 2048:2240]])
    slot = jnp.concatenate([slots[:4, :48].reshape(-1), slot_other[:, :48].reshape(-1)])
    pick_h = slot[:, None] == jnp.arange(512, dtype=jnp.int32)[None, :]
    ge_h = (
        lax.dot_general(
            jnp.where(pick_h, coeff[:, None], 0.0).astype(bf16),
            jnp.concatenate([block[:48] for block in back] + [pair_q_other], 0),
            (((0,), (0,)), ((), ())),
            preferred_element_type=f32,
        )
        * gain
        / normalizer_divisor
    )
    dot_h = jnp.sum(jnp.where(pick_h, pair_dot[:, None], 0.0), axis=0)
    grad_p = back_rows(p_vals, gain, p_scale, p_length, ge_p, dot_p)
    grad_h = back_rows(h_vals, gain, h_scale, h_length, ge_h, dot_h)
    ge_q = (
        pulled / z_own[:, None]
        + (e_own / z_own - 1.0)[:, None] * p_emb.astype(f32)
    ) / normalizer_divisor
    grad_q = back_rows(q_vals, gain, q_scale, q_length, ge_q, dot_q)
    return grad_q, grad_p, grad_h, packed[:16].reshape(-1), packed[16, 0] / 1024


def solution(mesh):
    return jax.shard_map(
        local,
        mesh=mesh,
        in_specs=(
            P("dp", "mp"),
            P("dp", "mp"),
            P("dp", "mp"),
            P("mp"),
            P("dp", None, None),
            P("dp", None),
        ),
        out_specs=(P("dp", "mp"), P("dp", "mp"), P("dp", "mp"), P("mp"), P()),
        check_vma=False,
    )
```

profile of v0, /device:TPU:1, one launch (start us, length us, event | category | flops | bytes accessed | tf_op | source)
XLA Modules:
  0.0 177.4 jit_solution(6880890935756453087)
XLA Ops:
  4.5 3.7 %collective-permute-start = (bf16[8,2176]{1,0:T(8,128)(2,1)S(1)}, bf16[8,2176]{1,0:T(8,128)(2,1)S(1)}, u32[]{:S(2)}, u32[]{:S(2)}) collective-permute-start(bf16[8,2176]{1,0:T(8,128)(2,1)S(1)} %pad_maximum_fusion.7), channel_id=1, source_target_pairs={{0,128},{2,130},{4,132},{6,134},{8,136},{10,138},{12,140},{14,142}... | collective-permute-start | bytes 104456 | tf_op jit(solution)/shard_map/ppermute | solution.py:20
  8.3 2.5 %fusion.3 = (f32[512]{0:T(512)S(1)}, f32[512]{0:T(512)S(1)}) fusion(bf16[512,2048]{1,0:T(8,128)(2,1)} %param.8, f32[2048]{0:T(1024)} %param.9), kind=kLoop, calls=%fused_computation.6 | loop fusion | flops 6290432 | bytes 2109440 | tf_op jit(solution)/shard_map/reduce_sum | solution.py:32
  11.1 7.0 %collective-permute-start.1 = (bf16[16,2176]{1,0:T(8,128)(2,1)S(1)}, bf16[16,2176]{1,0:T(8,128)(2,1)S(1)}, u32[]{:S(2)}, u32[]{:S(2)}) collective-permute-start(bf16[16,2176]{1,0:T(8,128)(2,1)S(1)} %pad_maximum_fusion.6), channel_id=1, source_target_pairs={{0,64},{2,66},{4,68},{6,70},{8,72},{10,74},{12,76},{14,78},{16,80}... | collective-permute-start | bytes 208904 | tf_op jit(solution)/shard_map/ppermute | solution.py:20
  18.5 2.4 %collective-permute-done.2 = f32[1040]{0:T(1024)S(1)} collective-permute-done((f32[1040]{0:T(1024)S(1)}, f32[1040]{0:T(1024)S(1)}, u32[]{:S(2)}, u32[]{:S(2)}) %collective-permute-start.2) | collective-permute-done | bytes 4192 | tf_op jit(solution)/shard_map/ppermute | solution.py:323
  24.6 5.0 %collective-permute-done.3 = bf16[32,2176]{1,0:T(8,128)(2,1)S(1)} collective-permute-done((bf16[32,2176]{1,0:T(8,128)(2,1)S(1)}, bf16[32,2176]{1,0:T(8,128)(2,1)S(1)}, u32[]{:S(2)}, u32[]{:S(2)}) %collective-permute-start.3) | collective-permute-done | bytes 139296 | tf_op jit(solution)/shard_map/ppermute | solution.py:20
  32.5 2.5 %collective-permute-start.6 = (bf16[8,2048]{1,0:T(8,128)(2,1)S(1)}, bf16[8,2048]{1,0:T(8,128)(2,1)S(1)}, u32[]{:S(2)}, u32[]{:S(2)}) collective-permute-start(bf16[8,2048]{1,0:T(8,128)(2,1)S(1)} %fusion.34), channel_id=1, source_target_pairs={{0,8},{2,10},{4,12},{6,14},{8,0},{10,2},{12,4},{14,6},{16,24},{18,... | collective-permute-start | bytes 98312 | tf_op jit(solution)/shard_map/ppermute | solution.py:20
  42.1 2.5 %collective-permute-start.11 = (bf16[128,128]{1,0:T(8,128)(2,1)S(1)}, bf16[128,128]{1,0:T(8,128)(2,1)S(1)}, u32[]{:S(2)}, u32[]{:S(2)}) collective-permute-start(bf16[128,128]{1,0:T(8,128)(2,1)S(1)} %get-tuple-element.142), channel_id=1, source_target_pairs={{0,8},{2,10},{4,12},{6,14},{8,0},{10,2},{12,4},{14,6},{16,24},{18,... | collective-permute-start | bytes 98312 | tf_op jit(solution)/shard_map/ppermute | solution.py:20
  44.8 2.7 %collective-permute-start.9 = (bf16[32,2048]{1,0:T(8,128)(2,1)}, bf16[32,2048]{1,0:T(8,128)(2,1)S(1)}, u32[]{:S(2)}, u32[]{:S(2)}) collective-permute-start(bf16[32,2048]{1,0:T(8,128)(2,1)} %pad_maximum_fusion.4), channel_id=1, source_target_pairs={{0,2},{2,0},{4,6},{6,4},{8,10},{10,8},{12,14},{14,12},{16,18},{18,... | collective-permute-start | bytes 393224 | tf_op jit(solution)/shard_map/ppermute | solution.py:20
  50.1 2.5 %shard_map.101 = (bf16[96,2048]{1,0:T(8,128)(2,1)S(1)}, bf16[96,2048]{1,0:T(8,128)(2,1)S(1)}, bf16[96,2048]{1,0:T(8,128)(2,1)S(1)}, bf16[96,2048]{1,0:T(8,128)(2...) custom-call(s32[1]{0:T(128)} %bitcast.1.me_ref, ...), custom_call_target="tpu_custom_call" | custom-call | tf_op jit(solution)/shard_map/pallas_call | solution.py:341
  57.5 3.2 %collective-permute-done.13.refs_5_.refs_1_ = bf16[96,2048]{1,0:T(8,128)(2,1)S(1)} collective-permute-done((bf16[96,2048]{1,0:T(8,128)(2,1)S(1)}, bf16[96,2048]{1,0:T(8,128)(2,1)S(1)}, u32[]{:S(2)}, u32[]{:S(2)}) %collective-permute-start.13) | collective-permute-done | bytes 393248 | tf_op jit(solution)/shard_map/ppermute | solution.py:20
  60.7 7.7 %collective-permute-done.14.refs_6_.refs_2_ = bf16[96,2048]{1,0:T(8,128)(2,1)S(1)} collective-permute-done((bf16[96,2048]{1,0:T(8,128)(2,1)S(1)}, bf16[96,2048]{1,0:T(8,128)(2,1)S(1)}, u32[]{:S(2)}, u32[]{:S(2)}) %collective-permute-start.14) | collective-permute-done | bytes 393248 | tf_op jit(solution)/shard_map/ppermute | solution.py:20
  71.0 2.7 %collective-permute-done.16.got = f32[72,128]{1,0:T(8,128)S(1)} collective-permute-done((f32[72,128]{1,0:T(8,128)S(1)}, f32[72,128]{1,0:T(8,128)S(1)}, u32[]{:S(2)}, u32[]{:S(2)}) %collective-permute-start.16) | collective-permute-done | bytes 36896 | tf_op jit(solution)/shard_map/ppermute | solution.py:354
  76.8 4.5 %collective-permute-done.17.got = bf16[80,2048]{1,0:T(8,128)(2,1)S(1)} collective-permute-done((bf16[80,2048]{1,0:T(8,128)(2,1)S(1)}, bf16[80,2048]{1,0:T(8,128)(2,1)S(1)}, u32[]{:S(2)}, u32[]{:S(2)}) %collective-permute-start.17) | collective-permute-done | bytes 327712 | tf_op jit(solution)/shard_map/ppermute | solution.py:20
  83.7 5.1 %collective-permute-done.18.got = bf16[48,2048]{1,0:T(8,128)(2,1)S(1)} collective-permute-done((bf16[48,2048]{1,0:T(8,128)(2,1)S(1)}, bf16[48,2048]{1,0:T(8,128)(2,1)S(1)}, u32[]{:S(2)}, u32[]{:S(2)}) %collective-permute-start.18) | collective-permute-done | bytes 196640 | tf_op jit(solution)/shard_map/ppermute | solution.py:20
  88.9 4.7 %collective-permute-start.19 = (bf16[32,2048]{1,0:T(8,128)(2,1)S(1)}, bf16[32,2048]{1,0:T(8,128)(2,1)S(1)}, u32[]{:S(2)}, u32[]{:S(2)}) collective-permute-start(bf16[32,2048]{1,0:T(8,128)(2,1)S(1)} %get-tuple-element.90), channel_id=1, source_target_pairs={{0,64},{2,66},{4,68},{6,70},{8,72},{10,74},{12,76},{14,78},{16,80}... | collective-permute-start | bytes 393224 | tf_op jit(solution)/shard_map/ppermute | solution.py:20
  93.7 12.7 %collective-permute-start.32 = (s32[4,128]{1,0:T(4,128)S(1)}, s32[4,128]{1,0:T(4,128)S(1)}, u32[]{:S(2)}, u32[]{:S(2)}) collective-permute-start(s32[4,128]{1,0:T(4,128)S(1)} %slice.190), channel_id=1, source_target_pairs={{0,2},{2,0},{4,6},{6,4},{8,10},{10,8},{12,14},{14,12},{16,18},{18,... | collective-permute-start | bytes 6152 | tf_op jit(solution)/shard_map/ppermute | solution.py:20
  106.4 3.8 %collective-permute-start.22 = (bf16[96,2048]{1,0:T(8,128)(2,1)}, bf16[96,2048]{1,0:T(8,128)(2,1)}, u32[]{:S(2)}, u32[]{:S(2)}) collective-permute-start(bf16[96,2048]{1,0:T(8,128)(2,1)} %get-tuple-element.75.refs_2_), channel_id=1, source_target_pairs={{0,8},{2,10},{4,12},{6,14},{8,0},{10,2},{12,4},{14,6},{16,24},{18,... | collective-permute-start | bytes 1179656 | tf_op jit(solution)/shard_map/ppermute | solution.py:20
  113.8 2.8 %collective-permute-done.20.got = f32[16,2048]{1,0:T(8,128)S(1)} collective-permute-done((f32[16,2048]{1,0:T(8,128)S(1)}, f32[16,2048]{1,0:T(8,128)S(1)}, u32[]{:S(2)}, u32[]{:S(2)}) %collective-permute-start.20) | collective-permute-done | bytes 131104 | tf_op jit(solution)/shard_map/ppermute | solution.py:20
  117.5 10.8 %collective-permute-done.22 = bf16[96,2048]{1,0:T(8,128)(2,1)} collective-permute-done((bf16[96,2048]{1,0:T(8,128)(2,1)}, bf16[96,2048]{1,0:T(8,128)(2,1)}, u32[]{:S(2)}, u32[]{:S(2)}) %collective-permute-start.22) | collective-permute-done | bytes 393248 | tf_op jit(solution)/shard_map/ppermute | solution.py:20
  130.3 2.6 %shard_map.108 = (f32[24,128]{1,0:T(8,128)S(1)}, f32[16,2176]{1,0:T(8,128)S(1)}, f32[16,2176]{1,0:T(8,128)S(1)}, f32[16,2176]{1,0:T(8,128)S(1)}, f32[16,2176]{1,0:T(8,128)S(1)}) custom-call(f32[8,128]{1,0:T(8,128)S(1)} %get-tuple-element.98.sums, f32[80,128]{1,0:T(8,128)S(1)} %get-tuple-element.82.small, s32[8,128]{1,0:T(8,128)S(1)} %get-tuple-element.81.query, ...), custom_call_target="tpu_custom_call" | custom-call | tf_op jit(solution)/shard_map/pallas_call | solution.py:366
  142.9 3.6 %collective-permute-done.26 = f32[24,128]{1,0:T(8,128)S(1)} collective-permute-done((f32[24,128]{1,0:T(8,128)S(1)}, f32[24,128]{1,0:T(8,128)S(1)}, u32[]{:S(2)}, u32[]{:S(2)}) %collective-permute-start.26) | collective-permute-done | bytes 12320 | tf_op jit(solution)/shard_map/ppermute | solution.py:20
  146.6 2.8 %collective-permute-done.29 = f32[16,2176]{1,0:T(8,128)S(1)} collective-permute-done((f32[16,2176]{1,0:T(8,128)S(1)}, f32[16,2176]{1,0:T(8,128)S(1)}, u32[]{:S(2)}, u32[]{:S(2)}) %collective-permute-start.29) | collective-permute-done | bytes 139296 | tf_op jit(solution)/shard_map/ppermute | solution.py:20
  159.8 4.2 %collective-permute-done.35 = f32[24,128]{1,0:T(8,128)S(1)} collective-permute-done((f32[24,128]{1,0:T(8,128)S(1)}, f32[24,128]{1,0:T(8,128)S(1)}, u32[]{:S(2)}, u32[]{:S(2)}) %collective-permute-start.35) | collective-permute-done | bytes 12320 | tf_op jit(solution)/shard_map/ppermute | solution.py:20
  170.8 5.5 %fusion.10 = bf16[512,2048]{1,0:T(8,128)(2,1)} fusion(bf16[512,2048]{1,0:T(8,128)(2,1)} %param.8, bf16[384,2048]{1,0:T(8,128)(2,1)} %constant_dynamic-update-slice_fusion.10, f32[512]{0:T(512)S(1)} %multiply_divide_fusion, f32[512]{0:T(512)S(1)} %select_reduce_fusion, f32[512]{0:T(512)S(1)} %fusion.48, f32[2048]{0:T(1024)S(1)} %copy-done.3, ...), kind=kOutput, calls=%fused_computation.13 | convolution fusion | flops 818282496 | bytes 5783808 | tf_op jit(solution)/shard_map/dot_general | solution.py:417
  (171 shorter events, 67.1 us)
Async XLA Ops:
  4.5 6.5 %collective-permute-start = (bf16[8,2176]{1,0:T(8,128)(2,1)S(1)}, bf16[8,2176]{1,0:T(8,128)(2,1)S(1)}, u32[]{:S(2)}, u32[]{:S(2)}) collective-permute-start(bf16[8,2176]{1,0:T(8,128)(2,1)S(1)} %pad_maximum_fusion.7), channel_id=1, source_target_pairs={{0,128},{2,130},{4,132},{6,134},{8,136},{10,138},{12,140},{14,142}... | collective-permute-start | bytes 104456 | tf_op jit(solution)/shard_map/ppermute | solution.py:20
  11.1 9.8 %collective-permute-start.1 = (bf16[16,2176]{1,0:T(8,128)(2,1)S(1)}, bf16[16,2176]{1,0:T(8,128)(2,1)S(1)}, u32[]{:S(2)}, u32[]{:S(2)}) collective-permute-start(bf16[16,2176]{1,0:T(8,128)(2,1)S(1)} %pad_maximum_fusion.6), channel_id=1, source_target_pairs={{0,64},{2,66},{4,68},{6,70},{8,72},{10,74},{12,76},{14,78},{16,80}... | collective-permute-start | bytes 208904 | tf_op jit(solution)/shard_map/ppermute | solution.py:20
  21.1 8.5 %collective-permute-start.3 = (bf16[32,2176]{1,0:T(8,128)(2,1)S(1)}, bf16[32,2176]{1,0:T(8,128)(2,1)S(1)}, u32[]{:S(2)}, u32[]{:S(2)}) collective-permute-start(bf16[32,2176]{1,0:T(8,128)(2,1)S(1)} %pad_maximum_fusion.3), channel_id=1, source_target_pairs={{0,32},{2,34},{4,36},{6,38},{8,40},{10,42},{12,44},{14,46},{16,48}... | collective-permute-start | bytes 417800 | tf_op jit(solution)/shard_map/ppermute | solution.py:20
  29.6 10.0 %collective-permute-start.8 = (bf16[512,2048]{1,0:T(8,128)(2,1)S(1)}, bf16[512,2048]{1,0:T(8,128)(2,1)S(1)}, u32[]{:S(2)}, u32[]{:S(2)}) collective-permute-start(bf16[512,2048]{1,0:T(8,128)(2,1)S(1)} %fusion.6.table_a), channel_id=1, source_target_pairs={{0,2},{2,0},{4,6},{6,4},{8,10},{10,8},{12,14},{14,12},{16,18},{18,... | collective-permute-start | bytes 6291464 | tf_op jit(solution)/shard_map/ppermute | solution.py:20
  31.2 8.3 %collective-permute-start.4 = (bf16[64,2176]{1,0:T(8,128)(2,1)S(1)}, bf16[64,2176]{1,0:T(8,128)(2,1)S(1)}, u32[]{:S(2)}, u32[]{:S(2)}) collective-permute-start(bf16[64,2176]{1,0:T(8,128)(2,1)S(1)} %pad_maximum_fusion.2), channel_id=1, source_target_pairs={{0,16},{2,18},{4,20},{6,22},{8,24},{10,26},{12,28},{14,30},{16,0},... | collective-permute-start | bytes 835592 | tf_op jit(solution)/shard_map/ppermute | solution.py:20
  40.9 6.6 %collective-permute-start.10 = (bf16[128,128]{1,0:T(8,128)(2,1)S(1)}, bf16[128,128]{1,0:T(8,128)(2,1)S(1)}, u32[]{:S(2)}, u32[]{:S(2)}) collective-permute-start(bf16[128,128]{1,0:T(8,128)(2,1)S(1)} %get-tuple-element.142), channel_id=1, source_target_pairs={{0,4},{2,6},{4,0},{6,2},{8,12},{10,14},{12,8},{14,10},{16,20},{18,... | collective-permute-start | bytes 98312 | tf_op jit(solution)/shard_map/ppermute | solution.py:20
  42.1 5.5 %collective-permute-start.11 = (bf16[128,128]{1,0:T(8,128)(2,1)S(1)}, bf16[128,128]{1,0:T(8,128)(2,1)S(1)}, u32[]{:S(2)}, u32[]{:S(2)}) collective-permute-start(bf16[128,128]{1,0:T(8,128)(2,1)S(1)} %get-tuple-element.142), channel_id=1, source_target_pairs={{0,8},{2,10},{4,12},{6,14},{8,0},{10,2},{12,4},{14,6},{16,24},{18,... | collective-permute-start | bytes 98312 | tf_op jit(solution)/shard_map/ppermute | solution.py:20
  44.8 12.6 %collective-permute-start.9 = (bf16[32,2048]{1,0:T(8,128)(2,1)}, bf16[32,2048]{1,0:T(8,128)(2,1)S(1)}, u32[]{:S(2)}, u32[]{:S(2)}) collective-permute-start(bf16[32,2048]{1,0:T(8,128)(2,1)} %pad_maximum_fusion.4), channel_id=1, source_target_pairs={{0,2},{2,0},{4,6},{6,4},{8,10},{10,8},{12,14},{14,12},{16,18},{18,... | collective-permute-start | bytes 393224 | tf_op jit(solution)/shard_map/ppermute | solution.py:20
  52.6 8.0 %collective-permute-start.13 = (bf16[96,2048]{1,0:T(8,128)(2,1)S(1)}, bf16[96,2048]{1,0:T(8,128)(2,1)S(1)}, u32[]{:S(2)}, u32[]{:S(2)}) collective-permute-start(bf16[96,2048]{1,0:T(8,128)(2,1)S(1)} %get-tuple-element.78), channel_id=1, source_target_pairs={{0,4},{2,6},{4,0},{6,2},{8,12},{10,14},{12,8},{14,10},{16,20},{18,... | collective-permute-start | bytes 1179656 | tf_op jit(solution)/shard_map/ppermute | solution.py:20
  52.6 15.7 %collective-permute-start.14 = (bf16[96,2048]{1,0:T(8,128)(2,1)S(1)}, bf16[96,2048]{1,0:T(8,128)(2,1)S(1)}, u32[]{:S(2)}, u32[]{:S(2)}) collective-permute-start(bf16[96,2048]{1,0:T(8,128)(2,1)S(1)} %get-tuple-element.79), channel_id=1, source_target_pairs={{0,8},{2,10},{4,12},{6,14},{8,0},{10,2},{12,4},{14,6},{16,24},{18,... | collective-permute-start | bytes 1179656 | tf_op jit(solution)/shard_map/ppermute | solution.py:20
  54.3 14.1 %collective-permute-start.15 = (bf16[96,2048]{1,0:T(8,128)(2,1)S(1)}, bf16[96,2048]{1,0:T(8,128)(2,1)S(1)}, u32[]{:S(2)}, u32[]{:S(2)}) collective-permute-start(bf16[96,2048]{1,0:T(8,128)(2,1)S(1)} %get-tuple-element.80), channel_id=1, source_target_pairs={{0,12},{2,14},{4,8},{6,10},{8,4},{10,6},{12,0},{14,2},{16,28},{18,... | collective-permute-start | bytes 1179656 | tf_op jit(solution)/shard_map/ppermute | solution.py:20
  74.7 6.6 %collective-permute-start.17 = (bf16[80,2048]{1,0:T(8,128)(2,1)S(1)}, bf16[80,2048]{1,0:T(8,128)(2,1)S(1)}, u32[]{:S(2)}, u32[]{:S(2)}) collective-permute-start(bf16[80,2048]{1,0:T(8,128)(2,1)S(1)} %get-tuple-element.84), channel_id=1, source_target_pairs={{0,16},{2,18},{4,20},{6,22},{8,24},{10,26},{12,28},{14,30},{16,0},... | collective-permute-start | bytes 983048 | tf_op jit(solution)/shard_map/ppermute | solution.py:20
  81.4 7.4 %collective-permute-start.18 = (bf16[48,2048]{1,0:T(8,128)(2,1)S(1)}, bf16[48,2048]{1,0:T(8,128)(2,1)S(1)}, u32[]{:S(2)}, u32[]{:S(2)}) collective-permute-start(bf16[48,2048]{1,0:T(8,128)(2,1)S(1)} %get-tuple-element.87), channel_id=1, source_target_pairs={{0,32},{2,34},{4,36},{6,38},{8,40},{10,42},{12,44},{14,46},{16,48}... | collective-permute-start | bytes 589832 | tf_op jit(solution)/shard_map/ppermute | solution.py:20
  88.9 22.2 %collective-permute-start.19 = (bf16[32,2048]{1,0:T(8,128)(2,1)S(1)}, bf16[32,2048]{1,0:T(8,128)(2,1)S(1)}, u32[]{:S(2)}, u32[]{:S(2)}) collective-permute-start(bf16[32,2048]{1,0:T(8,128)(2,1)S(1)} %get-tuple-element.90), channel_id=1, source_target_pairs={{0,64},{2,66},{4,68},{6,70},{8,72},{10,74},{12,76},{14,78},{16,80}... | collective-permute-start | bytes 393224 | tf_op jit(solution)/shard_map/ppermute | solution.py:20
  93.7 16.7 %collective-permute-start.32 = (s32[4,128]{1,0:T(4,128)S(1)}, s32[4,128]{1,0:T(4,128)S(1)}, u32[]{:S(2)}, u32[]{:S(2)}) collective-permute-start(s32[4,128]{1,0:T(4,128)S(1)} %slice.190), channel_id=1, source_target_pairs={{0,2},{2,0},{4,6},{6,4},{8,10},{10,8},{12,14},{14,12},{16,18},{18,... | collective-permute-start | bytes 6152 | tf_op jit(solution)/shard_map/ppermute | solution.py:20
  106.4 11.1 %collective-permute-start.21 = (bf16[96,2048]{1,0:T(8,128)(2,1)}, bf16[96,2048]{1,0:T(8,128)(2,1)}, u32[]{:S(2)}, u32[]{:S(2)}) collective-permute-start(bf16[96,2048]{1,0:T(8,128)(2,1)} %get-tuple-element.74.refs_1_), channel_id=1, source_target_pairs={{0,4},{2,6},{4,0},{6,2},{8,12},{10,14},{12,8},{14,10},{16,20},{18,... | collective-permute-start | bytes 1179656 | tf_op jit(solution)/shard_map/ppermute | solution.py:20
  106.4 21.8 %collective-permute-start.22 = (bf16[96,2048]{1,0:T(8,128)(2,1)}, bf16[96,2048]{1,0:T(8,128)(2,1)}, u32[]{:S(2)}, u32[]{:S(2)}) collective-permute-start(bf16[96,2048]{1,0:T(8,128)(2,1)} %get-tuple-element.75.refs_2_), channel_id=1, source_target_pairs={{0,8},{2,10},{4,12},{6,14},{8,0},{10,2},{12,4},{14,6},{16,24},{18,... | collective-permute-start | bytes 1179656 | tf_op jit(solution)/shard_map/ppermute | solution.py:20
  110.2 20.1 %collective-permute-start.23 = (bf16[96,2048]{1,0:T(8,128)(2,1)}, bf16[96,2048]{1,0:T(8,128)(2,1)}, u32[]{:S(2)}, u32[]{:S(2)}) collective-permute-start(bf16[96,2048]{1,0:T(8,128)(2,1)} %get-tuple-element.76.refs_3_), channel_id=1, source_target_pairs={{0,12},{2,14},{4,8},{6,10},{8,4},{10,6},{12,0},{14,2},{16,28},{18,... | collective-permute-start | bytes 1179656 | tf_op jit(solution)/shard_map/ppermute | solution.py:20
  111.2 5.4 %collective-permute-start.20 = (f32[16,2048]{1,0:T(8,128)S(1)}, f32[16,2048]{1,0:T(8,128)S(1)}, u32[]{:S(2)}, u32[]{:S(2)}) collective-permute-start(f32[16,2048]{1,0:T(8,128)S(1)} %get-tuple-element.93), channel_id=1, source_target_pairs={{0,128},{2,130},{4,132},{6,134},{8,136},{10,138},{12,140},{14,142}... | collective-permute-start | bytes 393224 | tf_op jit(solution)/shard_map/ppermute | solution.py:20
  137.8 32.0 %collective-permute-start.33 = (bf16[192,2048]{1,0:T(8,128)(2,1)S(1)}, bf16[192,2048]{1,0:T(8,128)(2,1)S(1)}, u32[]{:S(2)}, u32[]{:S(2)}) collective-permute-start(bf16[192,2048]{1,0:T(8,128)(2,1)S(1)} %pad_maximum_fusion), channel_id=1, source_target_pairs={{0,2},{2,0},{4,6},{6,4},{8,10},{10,8},{12,14},{14,12},{16,18},{18,... | collective-permute-start | bytes 2359304 | tf_op jit(solution)/shard_map/ppermute | solution.py:20
  137.9 8.7 %collective-permute-start.27 = (f32[16,2176]{1,0:T(8,128)S(1)}, f32[16,2176]{1,0:T(8,128)S(1)}, u32[]{:S(2)}, u32[]{:S(2)}) collective-permute-start(f32[16,2176]{1,0:T(8,128)S(1)} %get-tuple-element.106), channel_id=1, source_target_pairs={{0,4},{2,6},{4,0},{6,2},{8,12},{10,14},{12,8},{14,10},{16,20},{18,... | collective-permute-start | bytes 417800 | tf_op jit(solution)/shard_map/ppermute | solution.py:20
  139.6 6.9 %collective-permute-start.28 = (f32[16,2176]{1,0:T(8,128)S(1)}, f32[16,2176]{1,0:T(8,128)S(1)}, u32[]{:S(2)}, u32[]{:S(2)}) collective-permute-start(f32[16,2176]{1,0:T(8,128)S(1)} %get-tuple-element.107), channel_id=1, source_target_pairs={{0,8},{2,10},{4,12},{6,14},{8,0},{10,2},{12,4},{14,6},{16,24},{18,... | collective-permute-start | bytes 417800 | tf_op jit(solution)/shard_map/ppermute | solution.py:20
  139.6 9.8 %collective-permute-start.29 = (f32[16,2176]{1,0:T(8,128)S(1)}, f32[16,2176]{1,0:T(8,128)S(1)}, u32[]{:S(2)}, u32[]{:S(2)}) collective-permute-start(f32[16,2176]{1,0:T(8,128)S(1)} %get-tuple-element.108), channel_id=1, source_target_pairs={{0,12},{2,14},{4,8},{6,10},{8,4},{10,6},{12,0},{14,2},{16,28},{18,... | collective-permute-start | bytes 417800 | tf_op jit(solution)/shard_map/ppermute | solution.py:20
  157.5 6.5 %collective-permute-start.35 = (f32[24,128]{1,0:T(8,128)S(1)}, f32[24,128]{1,0:T(8,128)S(1)}, u32[]{:S(2)}, u32[]{:S(2)}) collective-permute-start(f32[24,128]{1,0:T(8,128)S(1)} %add.155), channel_id=1, source_target_pairs={{0,64},{2,66},{4,68},{6,70},{8,72},{10,74},{12,76},{14,78},{16,80}... | collective-permute-start | bytes 36872 | tf_op jit(solution)/shard_map/ppermute | solution.py:20
  (25 other events, 178.2 us)
where the time goes:
time: 181 us; the launch traced here: 177 us
  starting transfers between devices  68.8 us (38%)
  waiting for transfers between devices  68.7 us (38%)
  local copies, waits for them, and re-layouts  12 us (7%)
  other arithmetic  10.8 us (6%)
  Pallas kernels  8.63 us (5%)
  matrix products  5.68 us (3%)
  between operations  2.79 us (2%)
    ppermute x35, starting transfers between devices, flip(): return lax.ppermute(x, 'dp', [(i, i ^ mask) for i in range(128)])  68 us
    ppermute x35, waiting for transfers between devices, flip(): return lax.ppermute(x, 'dp', [(i, i ^ mask) for i in range(128)])  63.6 us
    dot_general x1, matrix products, local(): lax.dot_general(jnp.where(pick_h, coeff[:, None], 0.0).astype(bf16), jnp....  5.46 us
    unnamed x32, local copies, waits for them, and re-layouts  4.42 us
  transfers between devices with their start and end apart: 37, of which 20 were waited for; matrix products, arithmetic and copies ran while one was open for 8% of the time, Pallas kernels for 2%

commit v1 on v0

v1 whole, which is shorter than its diff:
```python
import functools

import jax
import jax.numpy as jnp
from jax import lax
from jax.experimental import pallas as pl
from jax.experimental.pallas import tpu as pltpu
from jax.sharding import PartitionSpec as P

D = 4096
normalizer_divisor = 0.02
eps_norm = 1e-06
f32 = jnp.float32
bf16 = jnp.bfloat16
C, X, Z, YH = 1, (2, 4), (8, 16, 32), 64
SWAP = [(0, 1), (1, 0)]


def flip(x, mask):
    return lax.ppermute(x, "dp", [(i, i ^ mask) for i in range(128)])


def double(x, mask):
    return jnp.concatenate([x, flip(x, mask)], 0)


def stats(values, gain):
    squares = values * values
    return jnp.sum(squares, axis=1), jnp.sum(squares * gain * gain, axis=1)


def scales(total_sq, total_gsq):
    scale = lax.rsqrt(total_sq / D + eps_norm)
    length = jnp.sqrt(scale * scale * total_gsq + eps_norm)
    return scale, length


def tie(*arrays):
    return lax.optimization_barrier(arrays)


def requests(hard_owner, hard_slot):
    owner = hard_owner.reshape(-1)
    slot = hard_slot.reshape(-1)
    number = jnp.arange(owner.shape[0], dtype=jnp.int32)
    earlier = (owner[:, None] == owner[None, :]) & (number[:, None] < number[None, :])
    position = jnp.sum(earlier.astype(jnp.int32), axis=0)
    low = slot % 256
    high = 1 + slot // 256 + 2 * (number // hard_slot.shape[1])
    place = jnp.arange(8, dtype=jnp.int32)[:, None]
    coded = jnp.where(
        place // 2 == position[None, :], jnp.where(place % 2 == 0, low[None, :], high[None, :]), 0
    ).astype(bf16)
    names = (owner[:, None] == jnp.arange(128, dtype=jnp.int32)[None, :]).astype(bf16)
    return jnp.dot(coded, names, preferred_element_type=f32).astype(bf16)


def diagonal(rows):
    shape = (rows, 128)
    return lax.broadcasted_iota(jnp.int32, shape, 0) == lax.broadcasted_iota(jnp.int32, shape, 1)


def as_row(column):
    return jnp.sum(jnp.where(diagonal(column.shape[0]), column, 0.0), axis=0, keepdims=True)


def as_column(row, rows):
    return jnp.sum(jnp.where(diagonal(rows), row, 0.0), axis=1, keepdims=True)


def score_kernel(panel, passages, gain, *refs):
    pair_q, near, out = refs[:4], refs[4:8], refs[8]
    g = gain[...]
    rows = panel[:, :2048]
    scaled = passages[...].astype(f32) * g
    high = scaled.astype(bf16)
    low = (scaled - high.astype(f32)).astype(bf16)
    contract = (((1,), (1,)), ((), ()))
    out[0:64] = lax.dot_general(
        high, rows, contract, preferred_element_type=f32
    ) + lax.dot_general(low, rows, contract, preferred_element_type=f32)
    values = rows.astype(f32)
    squares = values * values
    out[64:65] = as_row(jnp.sum(squares, axis=1, keepdims=True))
    out[65:66] = as_row(jnp.sum(squares * (g * g), axis=1, keepdims=True))
    for s in range(4):
        product = pair_q[s][...].astype(f32) * near[s][...].astype(f32) * g
        out[66 + s : 67 + s] = as_row(jnp.sum(product, axis=1, keepdims=True))
    out[70:72] = jnp.zeros((2, 128), f32)


def entry_columns(asked):
    row = lax.broadcasted_iota(jnp.int32, (96, 128), 0)
    entry = row >> 4
    entry = jnp.where(entry >= 3, 2 * entry - 5, 2 * entry)
    pick = (lax.broadcasted_iota(jnp.int32, (96, 128), 1) == (row & 15) * 8 + entry).astype(bf16)
    return jnp.dot(pick, asked, preferred_element_type=f32)


def decode(entries, column):
    lane = lax.broadcasted_iota(jnp.int32, (96, 128), 1)
    block = lax.broadcasted_iota(jnp.int32, (48, 1), 0) & 15
    values = jnp.sum(jnp.where(lane == column, entries, 0.0), axis=1, keepdims=True)
    low, high = values[:48].astype(jnp.int32), values[48:].astype(jnp.int32)
    slot = jnp.where(high > 0, low + 256 * ((high - 1) & 1), -1)
    return slot, jnp.where(high > 0, block * 8 + ((high - 1) >> 1), -1)


def row_of(index):
    return as_row((index + 1).astype(f32)).astype(jnp.int32) - 1


def one_hot(index, count):
    lanes = lax.broadcasted_iota(jnp.int32, (index.shape[0], count), 1)
    return (lanes == index).astype(f32)


def asker_kernel(me_ref, panel, *refs):
    pair_q, query = refs[:4], refs[4]
    me = me_ref[0]
    entries = entry_columns(panel[:, 2048:])
    for s in range(4):
        index = jnp.concatenate([decode(entries, me ^ (2 * s + t))[1] for t in range(2)], 0)
        query[s : s + 1] = row_of(index)
        pair_q[s][...] = jnp.dot(
            one_hot(index, 128).astype(bf16), panel[:, :2048], preferred_element_type=f32
        ).astype(bf16)
    query[4:8] = jnp.full((4, 128), -1, jnp.int32)


def owner_kernel(me_ref, panel, table_a, table_b, ratios, gain, *refs):
    asked, near, slots = refs[:3], refs[3:7], refs[7]
    me = me_ref[0]
    picks = ([], [])
    for s in range(4):
        entries = entry_columns(panel[:, 2048:] if s == 0 else asked[s - 1][...])
        both = [decode(entries, me ^ t)[0] for t in range(2)]
        for t in range(2):
            picks[t].append(one_hot(both[t], 512))
        slots[s : s + 1] = row_of(jnp.concatenate(both, 0))
    slots[4:8] = jnp.full((4, 128), -1, jnp.int32)
    for t, table in enumerate((table_a, table_b)):
        pick_h = jnp.concatenate(picks[t], 0)
        ratio = jnp.sum(jnp.where(pick_h > 0, ratios[t : t + 1], 0.0), axis=1, keepdims=True)
        values = jnp.dot(pick_h.astype(bf16), table[...], preferred_element_type=f32)
        values = (values * ratio * gain[...]).astype(bf16)
        for s in range(4):
            near[s][48 * t : 48 * t + 48] = values[48 * s : 48 * s + 48]


def split_sums(v):
    high = v.astype(bf16).astype(f32)
    middle = (v - high).astype(bf16).astype(f32)
    parts = [high, middle, v - high - middle, jnp.zeros((10, 128), f32)]
    return jnp.concatenate(parts, 0).astype(bf16)


def swap_lanes(v, bits):
    lane = lax.broadcasted_iota(jnp.int32, (8, 128), 1)
    for bit in (8, 16, 32, 64):
        if bits & bit:
            v = jnp.where(
                (lane & bit) > 0, pltpu.roll(v, bit, axis=1), pltpu.roll(v, 128 - bit, axis=1)
            )
    return v


def add_kernel(kept, sums, *refs):
    got, out, message, out_sums = refs[:7], refs[7], refs[8], refs[9]
    total = kept[...]
    v = sums[...]
    zeros = jnp.zeros((6, 128), f32)
    for m in range(1, 8):
        block = got[m - 1][...].astype(f32)
        total = total + block[:, :2048]
        extra = block[:, 2048:]
        extra = jnp.concatenate([extra[0:2] + extra[2:4] + extra[4:6], zeros], 0)
        v = v + swap_lanes(extra, 16 * m)
    out[...] = total[:8]
    message[0:8] = total[8:]
    message[8:16, :128] = v
    message[8:16, 128:] = jnp.zeros((8, 1920), f32)
    out_sums[...] = v


def late_kernel(slots, *refs):
    arrived, own, give, late, done = refs[:4], refs[4], refs[5], refs[6], refs[7]
    copies = [pltpu.make_async_copy(arrived[s], late.at[s], done.at[s]) for s in range(4)]
    for copy in copies:
        copy.start()
    for copy in copies:
        copy.wait()
    own[...] = sum(late[s, 0:8, :2048] for s in range(4))
    give[0:8, :2048] = sum(late[s, 8:16, :2048] for s in range(4))
    give[8:16, :2048] = jnp.zeros((8, 2048), f32)
    for s in range(4):
        give[s : s + 1, 2048:] = late[s, 0:1, 2048:]
        give[4 + s : 5 + s, 2048:] = late[s, 1:2, 2048:]
    give[8:9, 2048:] = sum(late[s, 2:3, 2048:] for s in range(4))
    give[9:13, 2048:] = slots[0:4].astype(f32)
    give[13:16, 2048:] = jnp.zeros((3, 128), f32)


def pack_kernel(*refs):
    back, other, rows, done = refs[:4], refs[4], refs[5], refs[6]
    copies = [
        pltpu.make_async_copy(back[s].at[48:96], rows.at[48 * s : 48 * s + 48], done.at[s])
        for s in range(4)
    ]
    for copy in copies:
        copy.start()
    for copy in copies:
        copy.wait()
    other[...] = rows[...]


def finish(values, ratio, tail, g, grad, dot):
    return (ratio * g * (grad - values * ratio * g * dot) - values * (tail * dot)).astype(bf16)


def hard_kernel(hidden_ref, passages, gain, totals, own_ref, give_ref, got_ref, *refs):
    back, other, out, out_p = refs[:4], refs[4], refs[5], refs[6]
    rows, hidden, own, give, got, done = refs[7:]
    copies = [
        pltpu.make_async_copy(own_ref, own, done.at[8]),
        pltpu.make_async_copy(give_ref, give, done.at[9]),
        pltpu.make_async_copy(got_ref, got, done.at[10]),
    ]
    for s in range(4):
        first, second = rows.at[128 * s : 128 * s + 48], rows.at[128 * s + 48 : 128 * s + 96]
        copies.append(pltpu.make_async_copy(back[s].at[0:48], first, done.at[2 * s]))
        copies.append(
            pltpu.make_async_copy(other.at[48 * s : 48 * s + 48], second, done.at[2 * s + 1])
        )
    pieces = [
        pltpu.make_async_copy(
            hidden_ref.at[128 * i : 128 * i + 128],
            hidden.at[128 * i : 128 * i + 128],
            done.at[11 + i],
        )
        for i in range(4)
    ]
    for copy in copies + pieces:
        copy.start()
    for s in range(4):
        rows[128 * s + 96 : 128 * s + 128] = jnp.zeros((32, 2048), bf16)
    for copy in copies:
        copy.wait()
    g = gain[...]
    inverse = g / normalizer_divisor
    lane = lax.broadcasted_iota(jnp.int32, (16, 128), 1)
    facts = jnp.where(lane < 48, give[:, 2048:], got[:, 2048:])
    scale = lax.rsqrt(totals[0:1] / D + eps_norm)
    length = jnp.sqrt(scale * scale * totals[1:2] + eps_norm)
    ratio = scale / length
    tail = scale * scale * eps_norm / (length * length * D)
    slot = jnp.concatenate([facts[9 + s : 10 + s] for s in range(4)], 1).astype(jnp.int32)
    coeff = jnp.concatenate([facts[s : s + 1] for s in range(4)], 1)
    pair_dot = jnp.concatenate([facts[4 + s : 5 + s] for s in range(4)], 1)
    used = (lax.broadcasted_iota(jnp.int32, (1, 512), 1) & 127) < 96
    slot = jnp.where(used, slot, -1)
    for i in range(4):
        pick = lax.broadcasted_iota(jnp.int32, (128, 512), 0) + 128 * i == slot
        weights = jnp.where(pick, coeff, 0.0).astype(bf16)
        grad = jnp.dot(weights, rows[...], preferred_element_type=f32)
        dot = jnp.sum(jnp.where(pick, pair_dot, 0.0), axis=1, keepdims=True)
        part = slice(128 * i, 128 * i + 128)
        pieces[i].wait()
        values = hidden[part, :].astype(f32)
        ratio_part, tail_part = as_column(ratio[:, part], 128), as_column(tail[:, part], 128)
        out[part, :] = finish(values, ratio_part, tail_part, g, grad * inverse, dot)
    row = give[8:16, 2048:] + pltpu.roll(got[8:16, 2048:], 120, axis=1)
    dot = as_column(row[0:1], 8)
    grad = (own[...] + got[0:8, :2048]) * inverse
    out_p[...] = finish(
        passages[...].astype(f32),
        as_column(ratio[:, 512:640], 8),
        as_column(tail[:, 512:640], 8),
        g,
        grad,
        dot,
    )


def pull_kernel(part, got, query, passages, *refs):
    near, kept, messages, sums, small = refs[:4], refs[4], refs[5:12], refs[12], refs[13]
    full = part[...] + got[...]
    scale = lax.rsqrt(full[64:65] / D + eps_norm)
    length = jnp.sqrt(scale * scale * full[65:66] + eps_norm)
    ratio = scale / length
    ratio_column = as_column(ratio, 128)
    s_in = full[:64] * ratio / normalizer_divisor
    e_in = jnp.exp(s_in)
    own = diagonal(64) & (lax.broadcasted_iota(jnp.int32, (64, 128), 0) < 8)
    total = lax.dot_general(
        jnp.where(own, 0.0, e_in).astype(bf16),
        passages[...],
        (((0,), (0,)), ((), ())),
        preferred_element_type=f32,
    )
    z = jnp.zeros((128, 1), f32)
    w = jnp.zeros((128, 1), f32)
    for s in range(4):
        asker = query[s : s + 1, :]
        pick = lax.broadcasted_iota(jnp.int32, (128, 128), 0) == asker
        ratio_pair = jnp.sum(jnp.where(pick, ratio_column, 0.0), axis=0, keepdims=True)
        s_pair = full[66 + s : 67 + s] * ratio_pair / normalizer_divisor
        e_pair = jnp.where(asker >= 0, jnp.exp(s_pair), 0.0)
        spread = jnp.where(pick, e_pair, 0.0)
        z = z + jnp.sum(spread, axis=1, keepdims=True)
        w = w + jnp.sum(spread * s_pair, axis=1, keepdims=True)
        total = total + jnp.dot(
            spread[:, :96].astype(bf16), near[s][...], preferred_element_type=f32
        )
        small[66 + s : 67 + s] = s_pair
        small[70 + s : 71 + s] = e_pair
        small[74 + s : 75 + s] = ratio_pair
    kept[...] = total[:16]
    small[0:64] = s_in
    z = jnp.sum(e_in, axis=0, keepdims=True) + as_row(z)
    w = jnp.sum(e_in * s_in, axis=0, keepdims=True) + as_row(w)
    v = jnp.concatenate([z, w], 0)
    extra = split_sums(v)
    for m in range(1, 8):
        messages[m - 1][:, :2048] = total[16 * m : 16 * m + 16].astype(bf16)
        messages[m - 1][:, 2048:] = extra
    sums[0:2] = v
    sums[2:8] = jnp.zeros((6, 128), f32)
    small[64:66] = v
    small[78:79] = scale
    small[79:80] = length


def weigh_kernel(kept, got, sums, small, query, panel, passages, gain, own_ref, *refs):
    pair_q, near, packed, late, out_q = refs[:4], refs[4:8], refs[8], refs[9:13], refs[13]
    g = gain[...]
    pulled = kept[...] + got[0:8]
    total = sums[...] + swap_lanes(got[8:16, :128], 8)
    z, w = total[0:1], total[1:2]
    s_in = small[0:64]
    scale, length = small[78:79], small[79:80]
    ratio = scale / length
    own = diagonal(64) & (lax.broadcasted_iota(jnp.int32, (64, 128), 0) < 8)
    c_in = ((jnp.exp(s_in) / z - jnp.where(own, 1.0, 0.0)) * ratio).astype(bf16)
    grads = jnp.dot(c_in, panel[:, :2048], preferred_element_type=f32)
    dots = jnp.sum(c_in.astype(f32) * (s_in / ratio), axis=1, keepdims=True)
    z_column = as_column(z, 128)
    values = passages[...].astype(f32)
    first = jnp.sum(grads * values, axis=0, keepdims=True)
    second = jnp.sum(values * values * dots, axis=0, keepdims=True)
    for s in range(4):
        asker = query[s : s + 1, :]
        pick = lax.broadcasted_iota(jnp.int32, (128, 128), 0) == asker
        z_pair = jnp.sum(jnp.where(pick, z_column, 0.0), axis=0, keepdims=True)
        c_pair = jnp.where(asker >= 0, small[70 + s : 71 + s] / z_pair, 0.0)
        ratio_pair = small[74 + s : 75 + s]
        coeff = (c_pair * ratio_pair).astype(bf16).astype(f32)
        pair_dot = jnp.where(asker >= 0, coeff * small[66 + s : 67 + s] / ratio_pair, 0.0)
        h = near[s][...].astype(f32)
        first = first + jnp.sum(
            pair_q[s][...].astype(f32) * h * as_column(coeff, 96), axis=0, keepdims=True
        )
        second = second + jnp.sum(h * h * as_column(pair_dot, 96), axis=0, keepdims=True)
        late[s][0:8, :2048] = grads[8 * s : 8 * s + 8]
        late[s][8:16, :2048] = grads[8 * s + 32 : 8 * s + 40]
        late[s][0:1, 2048:] = coeff
        late[s][1:2, 2048:] = pair_dot
        late[s][2:3, 2048:] = as_row(
            jnp.concatenate([dots[8 * s : 8 * s + 8], dots[8 * s + 32 : 8 * s + 40]], 0)
        )
        late[s][3:16, 2048:] = jnp.zeros((13, 128), f32)
    s_own = jnp.sum(jnp.where(own, s_in, 0.0), axis=0, keepdims=True)
    dot_own = as_column(w / z - s_own, 8)
    ratio_own = as_column(ratio, 8)
    values = own_ref[...].astype(f32)
    direct = values * ratio_own
    z_own = as_column(z, 8)
    excess = jnp.exp(as_column(s_own, 8)) / z_own - 1.0
    grad = (pulled / z_own + excess * passages[0:8].astype(f32)) / normalizer_divisor
    own_scale, own_length = as_column(scale, 8), as_column(length, 8)
    tail = own_scale * own_scale * eps_norm / (own_length * own_length * D)
    out_q[...] = finish(values, ratio_own, tail, g, grad, dot_own)
    third = jnp.sum(direct * direct * g * dot_own, axis=0, keepdims=True)
    result = first * (2.0 / normalizer_divisor) - second / g - third
    for i in range(16):
        packed[i : i + 1] = result[:, 128 * i : 128 * i + 128]
    lane = lax.broadcasted_iota(jnp.int32, (1, 128), 1)
    loss = jnp.sum(jnp.where(lane < 8, jnp.log(z) - s_own, 0.0), axis=1, keepdims=True)
    packed[16:24] = jnp.broadcast_to(loss, (8, 128))


def call(kernel, *shapes, scratch=(), limit=14, fetched=(), scalar=False):
    def run(*operands):
        spaces = [pltpu.HBM if own else pltpu.VMEM for own in fetched]
        spaces = spaces or [pltpu.SMEM if scalar and not i else pltpu.VMEM for i in range(len(operands))]
        return pl.pallas_call(
            kernel,
            out_shape=shapes,
            in_specs=[pl.BlockSpec(memory_space=space) for space in spaces],
            scratch_shapes=scratch,
            compiler_params=pltpu.CompilerParams(vmem_limit_bytes=limit * 1024 * 1024),
        )(*operands)

    return run


def local(query_hidden, passage_hidden, hard_hidden, gain, hard_owner, hard_slot):
    me = lax.axis_index("dp")
    p_vals = passage_hidden.astype(f32)
    h_vals = hard_hidden.astype(f32)
    p_sq, p_gsq = stats(p_vals, gain)
    h_sq, h_gsq = stats(h_vals, gain)
    mine = jnp.stack([jnp.concatenate([h_sq, p_sq]), jnp.concatenate([h_gsq, p_gsq])])
    mine = jnp.pad(mine, ((0, 0), (0, 120)))
    table = requests(hard_owner, hard_slot)
    panel = double(jnp.concatenate([query_hidden, table], 1), YH)
    panel, mine = tie(panel, mine)
    panel = double(panel, Z[2])
    tot = mine + lax.ppermute(mine, "mp", SWAP)
    panel, tot = tie(panel, tot)
    panel = double(panel, Z[1])
    scale, length = scales(tot[0], tot[1])
    p_scale, p_length = scale[512:520], length[512:520]
    h_scale, h_length = scale[:512], length[:512]
    p_emb = (p_vals * (p_scale / p_length)[:, None] * gain).astype(bf16)
    ratios = (h_scale / h_length)[None]
    panel, p_emb, hard_other = tie(panel, p_emb, flip(hard_hidden, C))
    panel = double(panel, Z[0])
    p_all = jnp.concatenate([p_emb] + [flip(p_emb, 2 * s) for s in (1, 2, 3)], 0)
    ratios = jnp.concatenate([ratios, flip(ratios, C)], 0)
    panel, p_all = tie(panel, p_all)
    wide = jax.ShapeDtypeStruct((96, 2048), bf16)
    index = jax.ShapeDtypeStruct((8, 128), jnp.int32)
    *pair_q, query = call(asker_kernel, *[wide] * 4, index, scalar=True)(me[None], panel)
    asked = panel[:, 2048:]
    asked = [flip(asked, 2 * s) for s in (1, 2, 3)]
    p_all = jnp.concatenate([p_all, flip(p_all, C)], 0)
    *near, slots = call(owner_kernel, *[wide] * 4, index, scalar=True, limit=20)(
        me[None], panel, hard_hidden, hard_other, ratios, gain[None], *asked
    )
    near = [near[0]] + [flip(near[s], 2 * s) for s in (1, 2, 3)]
    gain_row = gain[None]

    (part,) = call(score_kernel, jax.ShapeDtypeStruct((72, 128), f32))(
        panel, p_all, gain_row, *pair_q, *near
    )
    got = lax.ppermute(part, "mp", SWAP)
    kept, *messages, sums, small = call(
        pull_kernel,
        jax.ShapeDtypeStruct((16, 2048), f32),
        *[jax.ShapeDtypeStruct((16, 2176), bf16)] * 7,
        jax.ShapeDtypeStruct((8, 128), f32),
        jax.ShapeDtypeStruct((80, 128), f32),
    )(part, got, query, p_all, *near)
    messages = [flip(message, mask) for message, mask in zip(messages, (32, 16, 48, 8, 40, 24, 56))]
    kept, message, sums = call(
        add_kernel,
        jax.ShapeDtypeStruct((8, 2048), f32),
        jax.ShapeDtypeStruct((16, 2048), f32),
        jax.ShapeDtypeStruct((8, 128), f32),
    )(kept, sums, *messages)
    kept, message, sums, first, third = tie(kept, message, sums, pair_q[1], pair_q[3])
    first, third = flip(first, 2), flip(third, 6)
    packed, *late, grad_q = call(
        weigh_kernel,
        jax.ShapeDtypeStruct((24, 128), f32),
        *[jax.ShapeDtypeStruct((16, 2176), f32)] * 4,
        jax.ShapeDtypeStruct((8, 2048), bf16),
    )(
        kept,
        flip(message, YH),
        sums,
        small,
        query,
        panel,
        p_all,
        gain_row,
        query_hidden,
        *pair_q,
        *near,
    )
    late = [late[0]] + [flip(late[s], 2 * s) for s in (1, 2, 3)]
    packed = packed + flip(packed, Z[2])
    packed, first, third, second, *late = tie(packed, first, third, pair_q[2], *late)
    second = flip(second, 4)
    own, give = call(
        late_kernel,
        jax.ShapeDtypeStruct((8, 2048), f32),
        jax.ShapeDtypeStruct((16, 2176), f32),
        scratch=[pltpu.VMEM((4, 16, 2176), f32), pltpu.SemaphoreType.DMA((4,))],
        limit=4,
        fetched=[False] + [True] * 4,
    )(slots, *late)
    got = flip(give, C)
    packed = packed + flip(packed, YH)
    packed, got = tie(packed, got)
    packed = packed + flip(packed, Z[1])
    packed, second = tie(packed, second)
    back = [pair_q[0], first, second, third]
    (other,) = call(
        pack_kernel,
        jax.ShapeDtypeStruct((192, 2048), bf16),
        scratch=[pltpu.VMEM((192, 2048), bf16), pltpu.SemaphoreType.DMA((4,))],
        limit=4,
        fetched=[True] * 4,
    )(*back)
    other = flip(other, C)
    packed = packed + flip(packed, Z[0])
    packed, other = tie(packed, other)
    grad_h, grad_p = call(
        hard_kernel,
        jax.ShapeDtypeStruct((512, 2048), bf16),
        jax.ShapeDtypeStruct((8, 2048), bf16),
        scratch=[
            pltpu.VMEM((512, 2048), bf16),
            pltpu.VMEM((512, 2048), bf16),
            pltpu.VMEM((8, 2048), f32),
            pltpu.VMEM((16, 2176), f32),
            pltpu.VMEM((16, 2176), f32),
            pltpu.SemaphoreType.DMA((15,)),
        ],
        limit=60,
        fetched=[True, False, False, False] + [True] * 8,
    )(hard_hidden, passage_hidden, gain_row, tot, own, give, got, *back, other)
    for mask in X:
        packed = packed + flip(packed, mask)
    packed, grad_h = tie(packed, grad_h)
    packed = packed + flip(packed, C)
    return grad_q, grad_p, grad_h, packed[:16].reshape(-1), packed[16, 0] / 1024


def solution(mesh):
    return jax.shard_map(
        local,
        mesh=mesh,
        in_specs=(
            P("dp", "mp"),
            P("dp", "mp"),
            P("dp", "mp"),
            P("mp"),
            P("dp", None, None),
            P("dp", None),
        ),
        out_specs=(P("dp", "mp"), P("dp", "mp"), P("dp", "mp"), P("mp"), P()),
        check_vma=False,
    )
```

time: 181 us -> 164 us (0.906); the launches traced: 177 us -> 163 us
  waiting for transfers between devices: 68.7 us -> 58.7 us
  local copies, waits for them, and re-layouts: 12 us -> 2.56 us
  Pallas kernels: 8.63 us -> 17 us
  starting transfers between devices: 68.8 us -> 76.8 us
  other arithmetic: 10.8 us -> 5.23 us
  matrix products: 5.68 us -> 0.22 us
    ppermute x35 -> x39, waiting for transfers between devices: 63.6 us -> 53.3 us  [flip(): return lax.ppermute(x, 'dp', [(i, i ^ mask) for i in range(128)])]
    pallas_call x8 -> x9, Pallas kernels: 8.63 us -> 17 us  [run(): pl.pallas_call(kernel, out_shape=shapes, in_specs=[pl.BlockSpec(memory_sp...]
    ppermute x35 -> x39, starting transfers between devices: 68 us -> 76.2 us  [flip(): return lax.ppermute(x, 'dp', [(i, i ^ mask) for i in range(128)])]
    dot_general x1 -> x0, matrix products: 5.46 us -> none  [local(): lax.dot_general(jnp.where(pick_h, coeff[:, None], 0.0).astype(bf16), jnp....]
    unnamed x32 -> x28, local copies, waits for them, and re-layouts: 4.42 us -> 0.58 us
    slice x13 -> x1, local copies, waits for them, and re-layouts: 3.36 us -> 0.01 us  [local(): asked = panel[:, 2048:]]
    convert_element_type x2 -> x0, other arithmetic: 2.87 us -> none  [the longest x1 2.13 us: local(): h_emb = (h_vals * (h_scale / h_length)[:, None] * gain).astype(bf16)]
  transfers between devices with their start and end apart: 37 -> 41, of which waited for: 20 -> 19; matrix products, arithmetic and copies ran while one was open for 8% -> 2% of each run, Pallas kernels for 2% -> 8%
where the time goes in v1:
time: 164 us; the launch traced here: 163 us
  starting transfers between devices  76.8 us (47%)
  waiting for transfers between devices  58.7 us (36%)
  Pallas kernels  17 us (10%)
  other arithmetic  5.23 us (3%)
  between operations  2.85 us (2%)
  local copies, waits for them, and re-layouts  2.56 us (2%)
    ppermute x39, starting transfers between devices, flip(): return lax.ppermute(x, 'dp', [(i, i ^ mask) for i in range(128)])  76.2 us
    ppermute x39, waiting for transfers between devices, flip(): return lax.ppermute(x, 'dp', [(i, i ^ mask) for i in range(128)])  53.3 us
    pallas_call x9, Pallas kernels, run(): pl.pallas_call(kernel, out_shape=shapes, in_specs=[pl.BlockSpec(memory_sp...  17 us
  transfers between devices with their start and end apart: 41, of which 19 were waited for; matrix products, arithmetic and copies ran while one was open for 2% of the time, Pallas kernels for 8%

profile of v1, /device:TPU:1, one launch (start us, length us, event | category | flops | bytes accessed | tf_op | source)
XLA Modules:
  0.0 163.4 jit_solution(10066217528101030460)
XLA Ops:
  4.5 3.7 %collective-permute-start = (bf16[8,2176]{1,0:T(8,128)(2,1)S(1)}, bf16[8,2176]{1,0:T(8,128)(2,1)S(1)}, u32[]{:S(2)}, u32[]{:S(2)}) collective-permute-start(bf16[8,2176]{1,0:T(8,128)(2,1)S(1)} %pad_maximum_fusion.5), channel_id=1, source_target_pairs={{0,128},{2,130},{4,132},{6,134},{8,136},{10,138},{12,140},{14,142}... | collective-permute-start | bytes 104456 | tf_op jit(solution)/shard_map/ppermute | solution.py:20
  9.2 2.5 %fusion = (f32[512]{0:T(512)S(1)}, f32[512]{0:T(512)S(1)}) fusion(bf16[512,2048]{1,0:T(8,128)(2,1)} %hidden_ref.1, f32[2048]{0:T(1024)} %param.9), kind=kLoop, calls=%fused_computation.2 | loop fusion | flops 6290432 | bytes 2109440 | tf_op jit(solution)/shard_map/reduce_sum | solution.py:29
  12.1 7.0 %collective-permute-start.1 = (bf16[16,2176]{1,0:T(8,128)(2,1)S(1)}, bf16[16,2176]{1,0:T(8,128)(2,1)S(1)}, u32[]{:S(2)}, u32[]{:S(2)}) collective-permute-start(bf16[16,2176]{1,0:T(8,128)(2,1)S(1)} %pad_maximum_fusion.4), channel_id=1, source_target_pairs={{0,64},{2,66},{4,68},{6,70},{8,72},{10,74},{12,76},{14,78},{16,80}... | collective-permute-start | bytes 208904 | tf_op jit(solution)/shard_map/ppermute | solution.py:20
  19.4 2.3 %collective-permute-done.2 = f32[2,640]{1,0:T(2,128)S(1)} collective-permute-done((f32[2,640]{1,0:T(2,128)S(1)}, f32[2,640]{1,0:T(2,128)S(1)}, u32[]{:S(2)}, u32[]{:S(2)}) %collective-permute-start.2) | collective-permute-done | bytes 5152 | tf_op jit(solution)/shard_map/ppermute | solution.py:419
  21.8 2.6 %collective-permute-start.3 = (bf16[32,2176]{1,0:T(8,128)(2,1)S(1)}, bf16[32,2176]{1,0:T(8,128)(2,1)S(1)}, u32[]{:S(2)}, u32[]{:S(2)}) collective-permute-start(bf16[32,2176]{1,0:T(8,128)(2,1)S(1)} %pad_maximum_fusion.2), channel_id=1, source_target_pairs={{0,32},{2,34},{4,36},{6,38},{8,40},{10,42},{12,44},{14,46},{16,48}... | collective-permute-start | bytes 417800 | tf_op jit(solution)/shard_map/ppermute | solution.py:20
  24.6 6.7 %collective-permute-done.3 = bf16[32,2176]{1,0:T(8,128)(2,1)S(1)} collective-permute-done((bf16[32,2176]{1,0:T(8,128)(2,1)S(1)}, bf16[32,2176]{1,0:T(8,128)(2,1)S(1)}, u32[]{:S(2)}, u32[]{:S(2)}) %collective-permute-start.3) | collective-permute-done | bytes 139296 | tf_op jit(solution)/shard_map/ppermute | solution.py:20
  31.3 2.6 %collective-permute-start.8 = (bf16[8,2048]{1,0:T(8,128)(2,1)S(1)}, bf16[8,2048]{1,0:T(8,128)(2,1)S(1)}, u32[]{:S(2)}, u32[]{:S(2)}) collective-permute-start(bf16[8,2048]{1,0:T(8,128)(2,1)S(1)} %fusion.7), channel_id=1, source_target_pairs={{0,12},{2,14},{4,8},{6,10},{8,4},{10,6},{12,0},{14,2},{16,28},{18,... | collective-permute-start | bytes 98312 | tf_op jit(solution)/shard_map/ppermute | solution.py:20
  38.1 3.0 %collective-permute-done.5 = bf16[64,2176]{1,0:T(8,128)(2,1)S(1)} collective-permute-done((bf16[64,2176]{1,0:T(8,128)(2,1)S(1)}, bf16[64,2176]{1,0:T(8,128)(2,1)S(1)}, u32[]{:S(2)}, u32[]{:S(2)}) %collective-permute-start.5) | collective-permute-done | bytes 278560 | tf_op jit(solution)/shard_map/ppermute | solution.py:20
  41.1 2.6 %collective-permute-start.13 = (bf16[128,128]{1,0:T(8,128)(2,1)S(1)}, bf16[128,128]{1,0:T(8,128)(2,1)S(1)}, u32[]{:S(2)}, u32[]{:S(2)}) collective-permute-start(bf16[128,128]{1,0:T(8,128)(2,1)S(1)} %slice.41), channel_id=1, source_target_pairs={{0,12},{2,14},{4,8},{6,10},{8,4},{10,6},{12,0},{14,2},{16,28},{18,... | collective-permute-start | bytes 98312 | tf_op jit(solution)/shard_map/ppermute | solution.py:20
  44.5 3.5 %collective-permute-start.9 = (bf16[32,2048]{1,0:T(8,128)(2,1)S(1)}, bf16[32,2048]{1,0:T(8,128)(2,1)S(1)}, u32[]{:S(2)}, u32[]{:S(2)}) collective-permute-start(bf16[32,2048]{1,0:T(8,128)(2,1)S(1)} %pad_maximum_fusion.3), channel_id=1, source_target_pairs={{0,2},{2,0},{4,6},{6,4},{8,10},{10,8},{12,14},{14,12},{16,18},{18,... | collective-permute-start | bytes 393224 | tf_op jit(solution)/shard_map/ppermute | solution.py:20
  49.0 3.0 %shard_map.102 = (bf16[96,2048]{1,0:T(8,128)(2,1)S(1)}, bf16[96,2048]{1,0:T(8,128)(2,1)S(1)}, bf16[96,2048]{1,0:T(8,128)(2,1)S(1)}, bf16[96,2048]{1,0:T(8,128)(2,1)S(1)}, s32[8,128]{1,0:T(8,128)S(1)}) custom-call(s32[1]{0:T(128)} %bitcast.2.me_ref, bf16[128,2176]{1,0:T(8,128)(2,1)S(1)} %pad_maximum_fusion.panel, bf16[512,2048]{1,0:T(8,128)(2,1)S(1)} %copy-done, ...), custom_call_target="tpu_custom_call" | custom-call | tf_op jit(solution)/shard_map/pallas_call | solution.py:396
  53.4 2.5 %collective-permute-start.15 = (bf16[96,2048]{1,0:T(8,128)(2,1)S(1)}, bf16[96,2048]{1,0:T(8,128)(2,1)S(1)}, u32[]{:S(2)}, u32[]{:S(2)}) collective-permute-start(bf16[96,2048]{1,0:T(8,128)(2,1)S(1)} %get-tuple-element.83), channel_id=1, source_target_pairs={{0,8},{2,10},{4,12},{6,14},{8,0},{10,2},{12,4},{14,6},{16,24},{18,... | collective-permute-start | bytes 1179656 | tf_op jit(solution)/shard_map/ppermute | solution.py:20
  56.1 4.1 %collective-permute-done.14.refs_5_.refs_1_ = bf16[96,2048]{1,0:T(8,128)(2,1)S(1)} collective-permute-done((bf16[96,2048]{1,0:T(8,128)(2,1)S(1)}, bf16[96,2048]{1,0:T(8,128)(2,1)S(1)}, u32[]{:S(2)}, u32[]{:S(2)}) %collective-permute-start.14) | collective-permute-done | bytes 393248 | tf_op jit(solution)/shard_map/ppermute | solution.py:20
  60.1 11.8 %collective-permute-done.15.refs_6_.refs_2_ = bf16[96,2048]{1,0:T(8,128)(2,1)S(1)} collective-permute-done((bf16[96,2048]{1,0:T(8,128)(2,1)S(1)}, bf16[96,2048]{1,0:T(8,128)(2,1)S(1)}, u32[]{:S(2)}, u32[]{:S(2)}) %collective-permute-start.15) | collective-permute-done | bytes 393248 | tf_op jit(solution)/shard_map/ppermute | solution.py:20
  73.0 3.1 %collective-permute-done.17.got = f32[72,128]{1,0:T(8,128)S(1)} collective-permute-done((f32[72,128]{1,0:T(8,128)S(1)}, f32[72,128]{1,0:T(8,128)S(1)}, u32[]{:S(2)}, u32[]{:S(2)}) %collective-permute-start.17) | collective-permute-done | bytes 36896 | tf_op jit(solution)/shard_map/ppermute | solution.py:447
  77.1 5.2 %collective-permute-start.18 = (bf16[16,2176]{1,0:T(8,128)(2,1)S(1)}, bf16[16,2176]{1,0:T(8,128)(2,1)S(1)}, u32[]{:S(2)}, u32[]{:S(2)}) collective-permute-start(bf16[16,2176]{1,0:T(8,128)(2,1)S(1)} %get-tuple-element.88), channel_id=1, source_target_pairs={{0,64},{2,66},{4,68},{6,70},{8,72},{10,74},{12,76},{14,78},{16,80}... | collective-permute-start | bytes 208904 | tf_op jit(solution)/shard_map/ppermute | solution.py:20
  83.7 4.5 %collective-permute-start.22 = (bf16[16,2176]{1,0:T(8,128)(2,1)S(1)}, bf16[16,2176]{1,0:T(8,128)(2,1)S(1)}, u32[]{:S(2)}, u32[]{:S(2)}) collective-permute-start(bf16[16,2176]{1,0:T(8,128)(2,1)S(1)} %get-tuple-element.92), channel_id=1, source_target_pairs={{0,80},{2,82},{4,84},{6,86},{8,88},{10,90},{12,92},{14,94},{16,64}... | collective-permute-start | bytes 208904 | tf_op jit(solution)/shard_map/ppermute | solution.py:20
  89.8 3.7 %collective-permute-done.22.refs_4_ = bf16[16,2176]{1,0:T(8,128)(2,1)S(1)} collective-permute-done((bf16[16,2176]{1,0:T(8,128)(2,1)S(1)}, bf16[16,2176]{1,0:T(8,128)(2,1)S(1)}, u32[]{:S(2)}, u32[]{:S(2)}) %collective-permute-start.22) | collective-permute-done | bytes 69664 | tf_op jit(solution)/shard_map/ppermute | solution.py:20
  97.3 5.3 %collective-permute-done.25.got = f32[16,2048]{1,0:T(8,128)S(1)} collective-permute-done((f32[16,2048]{1,0:T(8,128)S(1)}, f32[16,2048]{1,0:T(8,128)S(1)}, u32[]{:S(2)}, u32[]{:S(2)}) %collective-permute-start.25) | collective-permute-done | bytes 131104 | tf_op jit(solution)/shard_map/ppermute | solution.py:20
  107.8 2.5 %collective-permute-start.30 = (f32[16,2176]{1,0:T(8,128)S(1)}, f32[16,2176]{1,0:T(8,128)S(1)}, u32[]{:S(2)}, u32[]{:S(2)}) collective-permute-start(f32[16,2176]{1,0:T(8,128)S(1)} %get-tuple-element.109), channel_id=1, source_target_pairs={{0,8},{2,10},{4,12},{6,14},{8,0},{10,2},{12,4},{14,6},{16,24},{18,... | collective-permute-start | bytes 417800 | tf_op jit(solution)/shard_map/ppermute | solution.py:20
  118.3 12.7 %collective-permute-start.33 = (f32[16,2176]{1,0:T(8,128)S(1)}, f32[16,2176]{1,0:T(8,128)S(1)}, u32[]{:S(2)}, u32[]{:S(2)}) collective-permute-start(f32[16,2176]{1,0:T(8,128)S(1)} %get-tuple-element.116.give_ref), channel_id=1, source_target_pairs={{0,2},{2,0},{4,6},{6,4},{8,10},{10,8},{12,14},{14,12},{16,18},{18,... | collective-permute-start | bytes 417800 | tf_op jit(solution)/shard_map/ppermute | solution.py:20
  131.0 4.4 %collective-permute-done.32 = f32[24,128]{1,0:T(8,128)S(1)} collective-permute-done((f32[24,128]{1,0:T(8,128)S(1)}, f32[24,128]{1,0:T(8,128)S(1)}, u32[]{:S(2)}, u32[]{:S(2)}) %collective-permute-start.32) | collective-permute-done | bytes 12320 | tf_op jit(solution)/shard_map/ppermute | solution.py:20
  149.9 6.9 %shard_map.109 = (bf16[512,2048]{1,0:T(8,128)(2,1)}, bf16[8,2048]{1,0:T(8,128)(2,1)}) custom-call(bf16[512,2048]{1,0:T(8,128)(2,1)} %hidden_ref.1, bf16[8,2048]{1,0:T(8,128)(2,1)} %passages.1, f32[1,2048]{1,0:T(1,128)} %bitcast.8, f32[2,640]{1,0:T(2,128)} %copy-done.12, f32[8,2048]{1,0:T(8,128)} %copy-done.8, f32[16,2176]{1,0:T(8,128)} %copy-done.7, ...), custom_call_target="tpu_custom_call" | custom-call | tf_op jit(solution)/shard_map/pallas_call | solution.py:396
  156.9 2.7 %collective-permute-start.40 = (f32[24,128]{1,0:T(8,128)S(1)}, f32[24,128]{1,0:T(8,128)S(1)}, u32[]{:S(2)}, u32[]{:S(2)}) collective-permute-start(f32[24,128]{1,0:T(8,128)S(1)} %add.97), channel_id=1, source_target_pairs={{0,2},{2,0},{4,6},{6,4},{8,10},{10,8},{12,14},{14,12},{16,18},{18,... | collective-permute-start | bytes 36872 | tf_op jit(solution)/shard_map/ppermute | solution.py:20
  (132 shorter events, 51.6 us)
Async XLA Ops:
  4.5 7.5 %collective-permute-start = (bf16[8,2176]{1,0:T(8,128)(2,1)S(1)}, bf16[8,2176]{1,0:T(8,128)(2,1)S(1)}, u32[]{:S(2)}, u32[]{:S(2)}) collective-permute-start(bf16[8,2176]{1,0:T(8,128)(2,1)S(1)} %pad_maximum_fusion.5), channel_id=1, source_target_pairs={{0,128},{2,130},{4,132},{6,134},{8,136},{10,138},{12,140},{14,142}... | collective-permute-start | bytes 104456 | tf_op jit(solution)/shard_map/ppermute | solution.py:20
  8.3 23.0 %collective-permute-start.4 = (bf16[512,2048]{1,0:T(8,128)(2,1)}, bf16[512,2048]{1,0:T(8,128)(2,1)}, u32[]{:S(2)}, u32[]{:S(2)}) collective-permute-start(bf16[512,2048]{1,0:T(8,128)(2,1)} %hidden_ref.1), channel_id=1, source_target_pairs={{0,2},{2,0},{4,6},{6,4},{8,10},{10,8},{12,14},{14,12},{16,18},{18,... | collective-permute-start | bytes 6291464 | tf_op jit(solution)/shard_map/ppermute | solution.py:20
  12.1 9.7 %collective-permute-start.1 = (bf16[16,2176]{1,0:T(8,128)(2,1)S(1)}, bf16[16,2176]{1,0:T(8,128)(2,1)S(1)}, u32[]{:S(2)}, u32[]{:S(2)}) collective-permute-start(bf16[16,2176]{1,0:T(8,128)(2,1)S(1)} %pad_maximum_fusion.4), channel_id=1, source_target_pairs={{0,64},{2,66},{4,68},{6,70},{8,72},{10,74},{12,76},{14,78},{16,80}... | collective-permute-start | bytes 208904 | tf_op jit(solution)/shard_map/ppermute | solution.py:20
  21.8 9.4 %collective-permute-start.3 = (bf16[32,2176]{1,0:T(8,128)(2,1)S(1)}, bf16[32,2176]{1,0:T(8,128)(2,1)S(1)}, u32[]{:S(2)}, u32[]{:S(2)}) collective-permute-start(bf16[32,2176]{1,0:T(8,128)(2,1)S(1)} %pad_maximum_fusion.2), channel_id=1, source_target_pairs={{0,32},{2,34},{4,36},{6,38},{8,40},{10,42},{12,44},{14,46},{16,48}... | collective-permute-start | bytes 417800 | tf_op jit(solution)/shard_map/ppermute | solution.py:20
  34.6 6.5 %collective-permute-start.5 = (bf16[64,2176]{1,0:T(8,128)(2,1)S(1)}, bf16[64,2176]{1,0:T(8,128)(2,1)S(1)}, u32[]{:S(2)}, u32[]{:S(2)}) collective-permute-start(bf16[64,2176]{1,0:T(8,128)(2,1)S(1)} %pad_maximum_fusion.1), channel_id=1, source_target_pairs={{0,16},{2,18},{4,20},{6,22},{8,24},{10,26},{12,28},{14,30},{16,0},... | collective-permute-start | bytes 835592 | tf_op jit(solution)/shard_map/ppermute | solution.py:20
  34.6 9.9 %collective-permute-start.10 = (f32[1,512]{1,0:T(1,128)S(1)}, f32[1,512]{1,0:T(1,128)S(1)}, u32[]{:S(2)}, u32[]{:S(2)}) collective-permute-start(f32[1,512]{1,0:T(1,128)S(1)} %slice_divide_fusion), channel_id=1, source_target_pairs={{0,2},{2,0},{4,6},{6,4},{8,10},{10,8},{12,14},{14,12},{16,18},{18,... | collective-permute-start | bytes 6152 | tf_op jit(solution)/shard_map/ppermute | solution.py:20
  41.1 7.8 %collective-permute-start.13 = (bf16[128,128]{1,0:T(8,128)(2,1)S(1)}, bf16[128,128]{1,0:T(8,128)(2,1)S(1)}, u32[]{:S(2)}, u32[]{:S(2)}) collective-permute-start(bf16[128,128]{1,0:T(8,128)(2,1)S(1)} %slice.41), channel_id=1, source_target_pairs={{0,12},{2,14},{4,8},{6,10},{8,4},{10,6},{12,0},{14,2},{16,28},{18,... | collective-permute-start | bytes 98312 | tf_op jit(solution)/shard_map/ppermute | solution.py:20
  44.5 11.6 %collective-permute-start.9 = (bf16[32,2048]{1,0:T(8,128)(2,1)S(1)}, bf16[32,2048]{1,0:T(8,128)(2,1)S(1)}, u32[]{:S(2)}, u32[]{:S(2)}) collective-permute-start(bf16[32,2048]{1,0:T(8,128)(2,1)S(1)} %pad_maximum_fusion.3), channel_id=1, source_target_pairs={{0,2},{2,0},{4,6},{6,4},{8,10},{10,8},{12,14},{14,12},{16,18},{18,... | collective-permute-start | bytes 393224 | tf_op jit(solution)/shard_map/ppermute | solution.py:20
  52.1 8.1 %collective-permute-start.14 = (bf16[96,2048]{1,0:T(8,128)(2,1)S(1)}, bf16[96,2048]{1,0:T(8,128)(2,1)S(1)}, u32[]{:S(2)}, u32[]{:S(2)}) collective-permute-start(bf16[96,2048]{1,0:T(8,128)(2,1)S(1)} %get-tuple-element.82), channel_id=1, source_target_pairs={{0,4},{2,6},{4,0},{6,2},{8,12},{10,14},{12,8},{14,10},{16,20},{18,... | collective-permute-start | bytes 1179656 | tf_op jit(solution)/shard_map/ppermute | solution.py:20
  53.4 18.5 %collective-permute-start.15 = (bf16[96,2048]{1,0:T(8,128)(2,1)S(1)}, bf16[96,2048]{1,0:T(8,128)(2,1)S(1)}, u32[]{:S(2)}, u32[]{:S(2)}) collective-permute-start(bf16[96,2048]{1,0:T(8,128)(2,1)S(1)} %get-tuple-element.83), channel_id=1, source_target_pairs={{0,8},{2,10},{4,12},{6,14},{8,0},{10,2},{12,4},{14,6},{16,24},{18,... | collective-permute-start | bytes 1179656 | tf_op jit(solution)/shard_map/ppermute | solution.py:20
  55.8 16.1 %collective-permute-start.16 = (bf16[96,2048]{1,0:T(8,128)(2,1)S(1)}, bf16[96,2048]{1,0:T(8,128)(2,1)S(1)}, u32[]{:S(2)}, u32[]{:S(2)}) collective-permute-start(bf16[96,2048]{1,0:T(8,128)(2,1)S(1)} %get-tuple-element.84), channel_id=1, source_target_pairs={{0,12},{2,14},{4,8},{6,10},{8,4},{10,6},{12,0},{14,2},{16,28},{18,... | collective-permute-start | bytes 1179656 | tf_op jit(solution)/shard_map/ppermute | solution.py:20
  77.1 11.2 %collective-permute-start.18 = (bf16[16,2176]{1,0:T(8,128)(2,1)S(1)}, bf16[16,2176]{1,0:T(8,128)(2,1)S(1)}, u32[]{:S(2)}, u32[]{:S(2)}) collective-permute-start(bf16[16,2176]{1,0:T(8,128)(2,1)S(1)} %get-tuple-element.88), channel_id=1, source_target_pairs={{0,64},{2,66},{4,68},{6,70},{8,72},{10,74},{12,76},{14,78},{16,80}... | collective-permute-start | bytes 208904 | tf_op jit(solution)/shard_map/ppermute | solution.py:20
  82.3 7.1 %collective-permute-start.19 = (bf16[16,2176]{1,0:T(8,128)(2,1)S(1)}, bf16[16,2176]{1,0:T(8,128)(2,1)S(1)}, u32[]{:S(2)}, u32[]{:S(2)}) collective-permute-start(bf16[16,2176]{1,0:T(8,128)(2,1)S(1)} %get-tuple-element.89), channel_id=1, source_target_pairs={{0,32},{2,34},{4,36},{6,38},{8,40},{10,42},{12,44},{14,46},{16,48}... | collective-permute-start | bytes 208904 | tf_op jit(solution)/shard_map/ppermute | solution.py:20
  82.3 7.5 %collective-permute-start.20 = (bf16[16,2176]{1,0:T(8,128)(2,1)S(1)}, bf16[16,2176]{1,0:T(8,128)(2,1)S(1)}, u32[]{:S(2)}, u32[]{:S(2)}) collective-permute-start(bf16[16,2176]{1,0:T(8,128)(2,1)S(1)} %get-tuple-element.90), channel_id=1, source_target_pairs={{0,96},{2,98},{4,100},{6,102},{8,104},{10,106},{12,108},{14,110},{... | collective-permute-start | bytes 208904 | tf_op jit(solution)/shard_map/ppermute | solution.py:20
  82.8 7.0 %collective-permute-start.21 = (bf16[16,2176]{1,0:T(8,128)(2,1)S(1)}, bf16[16,2176]{1,0:T(8,128)(2,1)S(1)}, u32[]{:S(2)}, u32[]{:S(2)}) collective-permute-start(bf16[16,2176]{1,0:T(8,128)(2,1)S(1)} %get-tuple-element.91), channel_id=1, source_target_pairs={{0,16},{2,18},{4,20},{6,22},{8,24},{10,26},{12,28},{14,30},{16,0},... | collective-permute-start | bytes 208904 | tf_op jit(solution)/shard_map/ppermute | solution.py:20
  83.7 9.7 %collective-permute-start.22 = (bf16[16,2176]{1,0:T(8,128)(2,1)S(1)}, bf16[16,2176]{1,0:T(8,128)(2,1)S(1)}, u32[]{:S(2)}, u32[]{:S(2)}) collective-permute-start(bf16[16,2176]{1,0:T(8,128)(2,1)S(1)} %get-tuple-element.92), channel_id=1, source_target_pairs={{0,80},{2,82},{4,84},{6,86},{8,88},{10,90},{12,92},{14,94},{16,64}... | collective-permute-start | bytes 208904 | tf_op jit(solution)/shard_map/ppermute | solution.py:20
  89.4 6.2 %collective-permute-start.24 = (bf16[16,2176]{1,0:T(8,128)(2,1)S(1)}, bf16[16,2176]{1,0:T(8,128)(2,1)S(1)}, u32[]{:S(2)}, u32[]{:S(2)}) collective-permute-start(bf16[16,2176]{1,0:T(8,128)(2,1)S(1)} %get-tuple-element.94), channel_id=1, source_target_pairs={{0,112},{2,114},{4,116},{6,118},{8,120},{10,122},{12,124},{14,126}... | collective-permute-start | bytes 208904 | tf_op jit(solution)/shard_map/ppermute | solution.py:20
  95.8 20.6 %collective-permute-start.27 = (bf16[96,2048]{1,0:T(8,128)(2,1)S(1)}, bf16[96,2048]{1,0:T(8,128)(2,1)S(1)}, u32[]{:S(2)}, u32[]{:S(2)}) collective-permute-start(bf16[96,2048]{1,0:T(8,128)(2,1)S(1)} %get-tuple-element.105.refs_1_), channel_id=1, source_target_pairs={{0,4},{2,6},{4,0},{6,2},{8,12},{10,14},{12,8},{14,10},{16,20},{18,... | collective-permute-start | bytes 1179656 | tf_op jit(solution)/shard_map/ppermute | solution.py:20
  95.8 20.5 %collective-permute-start.28 = (bf16[96,2048]{1,0:T(8,128)(2,1)S(1)}, bf16[96,2048]{1,0:T(8,128)(2,1)S(1)}, u32[]{:S(2)}, u32[]{:S(2)}) collective-permute-start(bf16[96,2048]{1,0:T(8,128)(2,1)S(1)} %get-tuple-element.106.refs_3_), channel_id=1, source_target_pairs={{0,12},{2,14},{4,8},{6,10},{8,4},{10,6},{12,0},{14,2},{16,28},{18,... | collective-permute-start | bytes 1179656 | tf_op jit(solution)/shard_map/ppermute | solution.py:20
  104.8 6.5 %collective-permute-start.26 = (f32[24,128]{1,0:T(8,128)S(1)}, f32[24,128]{1,0:T(8,128)S(1)}, u32[]{:S(2)}, u32[]{:S(2)}) collective-permute-start(f32[24,128]{1,0:T(8,128)S(1)} %get-tuple-element.104), channel_id=1, source_target_pairs={{0,64},{2,66},{4,68},{6,70},{8,72},{10,74},{12,76},{14,78},{16,80}... | collective-permute-start | bytes 36872 | tf_op jit(solution)/shard_map/ppermute | solution.py:20
  107.8 6.4 %collective-permute-start.30 = (f32[16,2176]{1,0:T(8,128)S(1)}, f32[16,2176]{1,0:T(8,128)S(1)}, u32[]{:S(2)}, u32[]{:S(2)}) collective-permute-start(f32[16,2176]{1,0:T(8,128)S(1)} %get-tuple-element.109), channel_id=1, source_target_pairs={{0,8},{2,10},{4,12},{6,14},{8,0},{10,2},{12,4},{14,6},{16,24},{18,... | collective-permute-start | bytes 417800 | tf_op jit(solution)/shard_map/ppermute | solution.py:20
  116.4 22.5 %collective-permute-start.35 = (bf16[96,2048]{1,0:T(8,128)(2,1)S(1)}, bf16[96,2048]{1,0:T(8,128)(2,1)S(1)}, u32[]{:S(2)}, u32[]{:S(2)}) collective-permute-start(bf16[96,2048]{1,0:T(8,128)(2,1)S(1)} %get-tuple-element.121.refs_2_), channel_id=1, source_target_pairs={{0,8},{2,10},{4,12},{6,14},{8,0},{10,2},{12,4},{14,6},{16,24},{18,... | collective-permute-start | bytes 1179656 | tf_op jit(solution)/shard_map/ppermute | solution.py:20
  118.3 17.0 %collective-permute-start.33 = (f32[16,2176]{1,0:T(8,128)S(1)}, f32[16,2176]{1,0:T(8,128)S(1)}, u32[]{:S(2)}, u32[]{:S(2)}) collective-permute-start(f32[16,2176]{1,0:T(8,128)S(1)} %get-tuple-element.116.give_ref), channel_id=1, source_target_pairs={{0,2},{2,0},{4,6},{6,4},{8,10},{10,8},{12,14},{14,12},{16,18},{18,... | collective-permute-start | bytes 417800 | tf_op jit(solution)/shard_map/ppermute | solution.py:20
  148.0 8.8 %collective-permute-start.39 = (f32[24,128]{1,0:T(8,128)S(1)}, f32[24,128]{1,0:T(8,128)S(1)}, u32[]{:S(2)}, u32[]{:S(2)}) collective-permute-start(f32[24,128]{1,0:T(8,128)S(1)} %add.96), channel_id=1, source_target_pairs={{0,8},{2,10},{4,12},{6,14},{8,0},{10,2},{12,4},{14,6},{16,24},{18,... | collective-permute-start | bytes 36872 | tf_op jit(solution)/shard_map/ppermute | solution.py:20
  (30 other events, 421.3 us)

commit v2 on v1

--- a/solution.py
+++ b/solution.py
@@ -68,11 +68,15 @@
     return jnp.sum(jnp.where(diagonal(rows), row, 0.0), axis=1, keepdims=True)
 
 
-def score_kernel(panel, passages, gain, *refs):
+def all_passages(near):
+    return jnp.concatenate([block[96:112] for block in near], 0)
+
+
+def score_kernel(panel, gain, *refs):
     pair_q, near, out = refs[:4], refs[4:8], refs[8]
     g = gain[...]
     rows = panel[:, :2048]
-    scaled = passages[...].astype(f32) * g
+    scaled = all_passages(near).astype(f32) * g
     high = scaled.astype(bf16)
     low = (scaled - high.astype(f32)).astype(bf16)
     contract = (((1,), (1,)), ((), ()))
@@ -84,7 +88,7 @@
     out[64:65] = as_row(jnp.sum(squares, axis=1, keepdims=True))
     out[65:66] = as_row(jnp.sum(squares * (g * g), axis=1, keepdims=True))
     for s in range(4):
-        product = pair_q[s][...].astype(f32) * near[s][...].astype(f32) * g
+        product = pair_q[s][...].astype(f32) * near[s][0:96].astype(f32) * g
         out[66 + s : 67 + s] = as_row(jnp.sum(product, axis=1, keepdims=True))
     out[70:72] = jnp.zeros((2, 128), f32)
 
@@ -128,12 +132,16 @@
     query[4:8] = jnp.full((4, 128), -1, jnp.int32)
 
 
-def owner_kernel(me_ref, panel, table_a, table_b, ratios, gain, *refs):
-    asked, near, slots = refs[:3], refs[3:7], refs[7]
+def owner_kernel(me_ref, panel, table_a, table_b, ratios, gain, p_a, p_b, *refs):
+    half, rest, near, slots = refs[0], refs[1], refs[2:6], refs[6]
     me = me_ref[0]
     picks = ([], [])
     for s in range(4):
-        entries = entry_columns(panel[:, 2048:] if s == 0 else asked[s - 1][...])
+        asked = panel[:, 2048:]
+        if s:
+            part = slice(64 * s - 64, 64 * s)
+            asked = jnp.concatenate([half[part], rest[part]], 0)
+        entries = entry_columns(asked)
         both = [decode(entries, me ^ t)[0] for t in range(2)]
         for t in range(2):
             picks[t].append(one_hot(both[t], 512))
@@ -146,6 +154,9 @@
         values = (values * ratio * gain[...]).astype(bf16)
         for s in range(4):
             near[s][48 * t : 48 * t + 48] = values[48 * s : 48 * s + 48]
+    both = jnp.concatenate([p_a[...].astype(f32), p_b[...].astype(f32)], 0).astype(bf16)
+    for s in range(4):
+        near[s][96:112] = both
 
 
 def split_sums(v):
@@ -282,7 +293,7 @@
     )
 
 
-def pull_kernel(part, got, query, passages, *refs):
+def pull_kernel(part, got, query, *refs):
     near, kept, messages, sums, small = refs[:4], refs[4], refs[5:12], refs[12], refs[13]
     full = part[...] + got[...]
     scale = lax.rsqrt(full[64:65] / D + eps_norm)
@@ -294,7 +305,7 @@
     own = diagonal(64) & (lax.broadcasted_iota(jnp.int32, (64, 128), 0) < 8)
     total = lax.dot_general(
         jnp.where(own, 0.0, e_in).astype(bf16),
-        passages[...],
+        all_passages(near),
         (((0,), (0,)), ((), ())),
         preferred_element_type=f32,
     )
@@ -310,7 +321,7 @@
         z = z + jnp.sum(spread, axis=1, keepdims=True)
         w = w + jnp.sum(spread * s_pair, axis=1, keepdims=True)
         total = total + jnp.dot(
-            spread[:, :96].astype(bf16), near[s][...], preferred_element_type=f32
+            spread[:, :96].astype(bf16), near[s][0:96], preferred_element_type=f32
         )
         small[66 + s : 67 + s] = s_pair
         small[70 + s : 71 + s] = e_pair
@@ -331,7 +342,7 @@
     small[79:80] = length
 
 
-def weigh_kernel(kept, got, sums, small, query, panel, passages, gain, own_ref, *refs):
+def weigh_kernel(kept, got, sums, small, query, panel, gain, own_ref, *refs):
     pair_q, near, packed, late, out_q = refs[:4], refs[4:8], refs[8], refs[9:13], refs[13]
     g = gain[...]
     pulled = kept[...] + got[0:8]
@@ -345,7 +356,8 @@
     grads = jnp.dot(c_in, panel[:, :2048], preferred_element_type=f32)
     dots = jnp.sum(c_in.astype(f32) * (s_in / ratio), axis=1, keepdims=True)
     z_column = as_column(z, 128)
-    values = passages[...].astype(f32)
+    values = all_passages(near).astype(f32)
+    p_own = values[0:8]
     first = jnp.sum(grads * values, axis=0, keepdims=True)
     second = jnp.sum(values * values * dots, axis=0, keepdims=True)
     for s in range(4):
@@ -356,18 +368,15 @@
         ratio_pair = small[74 + s : 75 + s]
         coeff = (c_pair * ratio_pair).astype(bf16).astype(f32)
         pair_dot = jnp.where(asker >= 0, coeff * small[66 + s : 67 + s] / ratio_pair, 0.0)
-        h = near[s][...].astype(f32)
+        h = near[s][0:96].astype(f32)
         first = first + jnp.sum(
             pair_q[s][...].astype(f32) * h * as_column(coeff, 96), axis=0, keepdims=True
         )
         second = second + jnp.sum(h * h * as_column(pair_dot, 96), axis=0, keepdims=True)
-        late[s][0:8, :2048] = grads[8 * s : 8 * s + 8]
-        late[s][8:16, :2048] = grads[8 * s + 32 : 8 * s + 40]
+        late[s][:, :2048] = grads[16 * s : 16 * s + 16]
         late[s][0:1, 2048:] = coeff
         late[s][1:2, 2048:] = pair_dot
-        late[s][2:3, 2048:] = as_row(
-            jnp.concatenate([dots[8 * s : 8 * s + 8], dots[8 * s + 32 : 8 * s + 40]], 0)
-        )
+        late[s][2:3, 2048:] = as_row(dots[16 * s : 16 * s + 16])
         late[s][3:16, 2048:] = jnp.zeros((13, 128), f32)
     s_own = jnp.sum(jnp.where(own, s_in, 0.0), axis=0, keepdims=True)
     dot_own = as_column(w / z - s_own, 8)
@@ -376,7 +385,7 @@
     direct = values * ratio_own
     z_own = as_column(z, 8)
     excess = jnp.exp(as_column(s_own, 8)) / z_own - 1.0
-    grad = (pulled / z_own + excess * passages[0:8].astype(f32)) / normalizer_divisor
+    grad = (pulled / z_own + excess * p_own) / normalizer_divisor
     own_scale, own_length = as_column(scale, 8), as_column(length, 8)
     tail = own_scale * own_scale * eps_norm / (own_length * own_length * D)
     out_q[...] = finish(values, ratio_own, tail, g, grad, dot_own)
@@ -425,24 +434,24 @@
     p_emb = (p_vals * (p_scale / p_length)[:, None] * gain).astype(bf16)
     ratios = (h_scale / h_length)[None]
     panel, p_emb, hard_other = tie(panel, p_emb, flip(hard_hidden, C))
+    half = jnp.concatenate([flip(panel[:, 2048:], 2 * s) for s in (1, 2, 3)], 0)
+    rest = flip(half, Z[0])
     panel = double(panel, Z[0])
-    p_all = jnp.concatenate([p_emb] + [flip(p_emb, 2 * s) for s in (1, 2, 3)], 0)
+    p_other = flip(p_emb, C)
     ratios = jnp.concatenate([ratios, flip(ratios, C)], 0)
-    panel, p_all = tie(panel, p_all)
+    panel, half, rest, p_other = tie(panel, half, rest, p_other)
     wide = jax.ShapeDtypeStruct((96, 2048), bf16)
     index = jax.ShapeDtypeStruct((8, 128), jnp.int32)
     *pair_q, query = call(asker_kernel, *[wide] * 4, index, scalar=True)(me[None], panel)
-    asked = panel[:, 2048:]
-    asked = [flip(asked, 2 * s) for s in (1, 2, 3)]
-    p_all = jnp.concatenate([p_all, flip(p_all, C)], 0)
-    *near, slots = call(owner_kernel, *[wide] * 4, index, scalar=True, limit=20)(
-        me[None], panel, hard_hidden, hard_other, ratios, gain[None], *asked
+    deep = jax.ShapeDtypeStruct((112, 2048), bf16)
+    *near, slots = call(owner_kernel, *[deep] * 4, index, scalar=True, limit=20)(
+        me[None], panel, hard_hidden, hard_other, ratios, gain[None], p_emb, p_other, half, rest
     )
     near = [near[0]] + [flip(near[s], 2 * s) for s in (1, 2, 3)]
     gain_row = gain[None]
 
     (part,) = call(score_kernel, jax.ShapeDtypeStruct((72, 128), f32))(
-        panel, p_all, gain_row, *pair_q, *near
+        panel, gain_row, *pair_q, *near
     )
     got = lax.ppermute(part, "mp", SWAP)
     kept, *messages, sums, small = call(
@@ -451,7 +460,7 @@
         *[jax.ShapeDtypeStruct((16, 2176), bf16)] * 7,
         jax.ShapeDtypeStruct((8, 128), f32),
         jax.ShapeDtypeStruct((80, 128), f32),
-    )(part, got, query, p_all, *near)
+    )(part, got, query, *near)
     messages = [flip(message, mask) for message, mask in zip(messages, (32, 16, 48, 8, 40, 24, 56))]
     kept, message, sums = call(
         add_kernel,
@@ -473,7 +482,6 @@
         small,
         query,
         panel,
-        p_all,
         gain_row,
         query_hidden,
         *pair_q,
@@ -481,8 +489,7 @@
     )
     late = [late[0]] + [flip(late[s], 2 * s) for s in (1, 2, 3)]
     packed = packed + flip(packed, Z[2])
-    packed, first, third, second, *late = tie(packed, first, third, pair_q[2], *late)
-    second = flip(second, 4)
+    packed, *late = tie(packed, *late)
     own, give = call(
         late_kernel,
         jax.ShapeDtypeStruct((8, 2048), f32),
@@ -493,8 +500,10 @@
     )(slots, *late)
     got = flip(give, C)
     packed = packed + flip(packed, YH)
-    packed, got = tie(packed, got)
-    packed = packed + flip(packed, Z[1])
+    packed, got, first, third, second = tie(packed, got, first, third, pair_q[2])
+    second = flip(second, 4)
+    for mask in (Z[1], Z[0]):
+        packed = packed + flip(packed, mask)
     packed, second = tie(packed, second)
     back = [pair_q[0], first, second, third]
     (other,) = call(
@@ -505,7 +514,7 @@
         fetched=[True] * 4,
     )(*back)
     other = flip(other, C)
-    packed = packed + flip(packed, Z[0])
+    packed = packed + flip(packed, X[0])
     packed, other = tie(packed, other)
     grad_h, grad_p = call(
         hard_kernel,
@@ -522,8 +531,7 @@
         limit=60,
         fetched=[True, False, False, False] + [True] * 8,
     )(hard_hidden, passage_hidden, gain_row, tot, own, give, got, *back, other)
-    for mask in X:
-        packed = packed + flip(packed, mask)
+    packed = packed + flip(packed, X[1])
     packed, grad_h = tie(packed, grad_h)
     packed = packed + flip(packed, C)
     return grad_q, grad_p, grad_h, packed[:16].reshape(-1), packed[16, 0] / 1024

time: 164 us -> 159 us (0.970)
  starting transfers between devices: 76.8 us -> 69.5 us
  waiting for transfers between devices: 58.7 us -> 61 us
    ppermute x39 -> x37, starting transfers between devices: 76.2 us -> 68.2 us  [flip(): return lax.ppermute(x, 'dp', [(i, i ^ mask) for i in range(128)])]
    ppermute x39 -> x37, waiting for transfers between devices: 53.3 us -> 56.3 us  [flip(): return lax.ppermute(x, 'dp', [(i, i ^ mask) for i in range(128)])]
  transfers between devices with their start and end apart: 41 -> 39, of which waited for: 19 -> 21; matrix products, arithmetic and copies ran while one was open for 2% -> 2% of each run, Pallas kernels for 8% -> 7%
where the time goes in v2:
time: 159 us; the launch traced here: 158 us
  starting transfers between devices  69.5 us (44%)
  waiting for transfers between devices  61 us (38%)
  Pallas kernels  16.9 us (11%)
  other arithmetic  5.22 us (3%)
  between operations  2.8 us (2%)
  local copies, waits for them, and re-layouts  2.65 us (2%)
    ppermute x37, starting transfers between devices, flip(): return lax.ppermute(x, 'dp', [(i, i ^ mask) for i in range(128)])  68.2 us
    ppermute x37, waiting for transfers between devices, flip(): return lax.ppermute(x, 'dp', [(i, i ^ mask) for i in range(128)])  56.3 us
    pallas_call x9, Pallas kernels, run(): pl.pallas_call(kernel, out_shape=shapes, in_specs=[pl.BlockSpec(memory_sp...  16.9 us
  transfers between devices with their start and end apart: 39, of which 21 were waited for; matrix products, arithmetic and copies ran while one was open for 2% of the time, Pallas kernels for 7%

profile of v2, /device:TPU:1, one launch (start us, length us, event | category | flops | bytes accessed | tf_op | source)
XLA Modules:
  0.0 158.2 jit_solution(2396811626163846487)
XLA Ops:
  4.5 3.7 %collective-permute-start = (bf16[8,2176]{1,0:T(8,128)(2,1)S(1)}, bf16[8,2176]{1,0:T(8,128)(2,1)S(1)}, u32[]{:S(2)}, u32[]{:S(2)}) collective-permute-start(bf16[8,2176]{1,0:T(8,128)(2,1)S(1)} %pad_maximum_fusion.4), channel_id=1, source_target_pairs={{0,128},{2,130},{4,132},{6,134},{8,136},{10,138},{12,140},{14,142}... | collective-permute-start | bytes 104456 | tf_op jit(solution)/shard_map/ppermute | solution.py:20
  9.2 2.5 %fusion = (f32[512]{0:T(512)S(1)}, f32[512]{0:T(512)S(1)}) fusion(bf16[512,2048]{1,0:T(8,128)(2,1)} %hidden_ref.1, f32[2048]{0:T(1024)} %param.9), kind=kLoop, calls=%fused_computation.2 | loop fusion | flops 6290432 | bytes 2109440 | tf_op jit(solution)/shard_map/reduce_sum | solution.py:29
  12.0 7.0 %collective-permute-start.1 = (bf16[16,2176]{1,0:T(8,128)(2,1)S(1)}, bf16[16,2176]{1,0:T(8,128)(2,1)S(1)}, u32[]{:S(2)}, u32[]{:S(2)}) collective-permute-start(bf16[16,2176]{1,0:T(8,128)(2,1)S(1)} %pad_maximum_fusion.3), channel_id=1, source_target_pairs={{0,64},{2,66},{4,68},{6,70},{8,72},{10,74},{12,76},{14,78},{16,80}... | collective-permute-start | bytes 208904 | tf_op jit(solution)/shard_map/ppermute | solution.py:20
  19.4 2.3 %collective-permute-done.2 = f32[2,640]{1,0:T(2,128)S(1)} collective-permute-done((f32[2,640]{1,0:T(2,128)S(1)}, f32[2,640]{1,0:T(2,128)S(1)}, u32[]{:S(2)}, u32[]{:S(2)}) %collective-permute-start.2) | collective-permute-done | bytes 5152 | tf_op jit(solution)/shard_map/ppermute | solution.py:428
  23.1 2.3 %collective-permute-start.3 = (bf16[32,2176]{1,0:T(8,128)(2,1)S(1)}, bf16[32,2176]{1,0:T(8,128)(2,1)S(1)}, u32[]{:S(2)}, u32[]{:S(2)}) collective-permute-start(bf16[32,2176]{1,0:T(8,128)(2,1)S(1)} %pad_maximum_fusion.2), channel_id=1, source_target_pairs={{0,32},{2,34},{4,36},{6,38},{8,40},{10,42},{12,44},{14,46},{16,48}... | collective-permute-start | bytes 417800 | tf_op jit(solution)/shard_map/ppermute | solution.py:20
  25.5 6.7 %collective-permute-done.3 = bf16[32,2176]{1,0:T(8,128)(2,1)S(1)} collective-permute-done((bf16[32,2176]{1,0:T(8,128)(2,1)S(1)}, bf16[32,2176]{1,0:T(8,128)(2,1)S(1)}, u32[]{:S(2)}, u32[]{:S(2)}) %collective-permute-start.3) | collective-permute-done | bytes 139296 | tf_op jit(solution)/shard_map/ppermute | solution.py:20
  39.7 3.3 %collective-permute-done.5 = bf16[64,2176]{1,0:T(8,128)(2,1)S(1)} collective-permute-done((bf16[64,2176]{1,0:T(8,128)(2,1)S(1)}, bf16[64,2176]{1,0:T(8,128)(2,1)S(1)}, u32[]{:S(2)}, u32[]{:S(2)}) %collective-permute-start.5) | collective-permute-done | bytes 278560 | tf_op jit(solution)/shard_map/ppermute | solution.py:20
  44.0 2.9 %shard_map.102 = (bf16[112,2048]{1,0:T(8,128)(2,1)S(1)}, bf16[112,2048]{1,0:T(8,128)(2,1)S(1)}, bf16[112,2048]{1,0:T(8,128)(2,1)S(1)}, bf16[112,2048]{1,0:T(8,128)(2,1)S(1)}, s32[8,128]{1,0:T(8,128)S(1)}) custom-call(s32[1]{0:T(128)} %bitcast.2.me_ref, bf16[128,2176]{1,0:T(8,128)(2,1)S(1)} %pad_maximum_fusion.panel, bf16[512,2048]{1,0:T(8,128)(2,1)S(1)} %copy-done, ...), custom_call_target="tpu_custom_call" | custom-call | tf_op jit(solution)/shard_map/pallas_call | solution.py:405
  47.5 2.5 %collective-permute-start.13 = (bf16[112,2048]{1,0:T(8,128)(2,1)S(1)}, bf16[112,2048]{1,0:T(8,128)(2,1)S(1)}, u32[]{:S(2)}, u32[]{:S(2)}) collective-permute-start(bf16[112,2048]{1,0:T(8,128)(2,1)S(1)} %get-tuple-element.87), channel_id=1, source_target_pairs={{0,8},{2,10},{4,12},{6,14},{8,0},{10,2},{12,4},{14,6},{16,24},{18,... | collective-permute-start | bytes 1376264 | tf_op jit(solution)/shard_map/ppermute | solution.py:20
  51.9 4.8 %collective-permute-done.12.refs_5_.refs_1_ = bf16[112,2048]{1,0:T(8,128)(2,1)S(1)} collective-permute-done((bf16[112,2048]{1,0:T(8,128)(2,1)S(1)}, bf16[112,2048]{1,0:T(8,128)(2,1)S(1)}, u32[]{:S(2)}, u32[]{:S(2)}) %collective-permute-start.12) | collective-permute-done | bytes 458784 | tf_op jit(solution)/shard_map/ppermute | solution.py:20
  56.7 11.0 %collective-permute-done.13.refs_6_.refs_2_ = bf16[112,2048]{1,0:T(8,128)(2,1)S(1)} collective-permute-done((bf16[112,2048]{1,0:T(8,128)(2,1)S(1)}, bf16[112,2048]{1,0:T(8,128)(2,1)S(1)}, u32[]{:S(2)}, u32[]{:S(2)}) %collective-permute-start.13) | collective-permute-done | bytes 458784 | tf_op jit(solution)/shard_map/ppermute | solution.py:20
  69.5 2.4 %collective-permute-done.15.got = f32[72,128]{1,0:T(8,128)S(1)} collective-permute-done((f32[72,128]{1,0:T(8,128)S(1)}, f32[72,128]{1,0:T(8,128)S(1)}, u32[]{:S(2)}, u32[]{:S(2)}) %collective-permute-start.15) | collective-permute-done | bytes 36896 | tf_op jit(solution)/shard_map/ppermute | solution.py:456
  72.9 5.4 %collective-permute-start.16 = (bf16[16,2176]{1,0:T(8,128)(2,1)S(1)}, bf16[16,2176]{1,0:T(8,128)(2,1)S(1)}, u32[]{:S(2)}, u32[]{:S(2)}) collective-permute-start(bf16[16,2176]{1,0:T(8,128)(2,1)S(1)} %get-tuple-element.92), channel_id=1, source_target_pairs={{0,64},{2,66},{4,68},{6,70},{8,72},{10,74},{12,76},{14,78},{16,80}... | collective-permute-start | bytes 208904 | tf_op jit(solution)/shard_map/ppermute | solution.py:20
  79.9 4.4 %collective-permute-start.20 = (bf16[16,2176]{1,0:T(8,128)(2,1)S(1)}, bf16[16,2176]{1,0:T(8,128)(2,1)S(1)}, u32[]{:S(2)}, u32[]{:S(2)}) collective-permute-start(bf16[16,2176]{1,0:T(8,128)(2,1)S(1)} %get-tuple-element.96), channel_id=1, source_target_pairs={{0,80},{2,82},{4,84},{6,86},{8,88},{10,90},{12,92},{14,94},{16,64}... | collective-permute-start | bytes 208904 | tf_op jit(solution)/shard_map/ppermute | solution.py:20
  86.2 4.1 %collective-permute-done.21.refs_5_ = bf16[16,2176]{1,0:T(8,128)(2,1)S(1)} collective-permute-done((bf16[16,2176]{1,0:T(8,128)(2,1)S(1)}, bf16[16,2176]{1,0:T(8,128)(2,1)S(1)}, u32[]{:S(2)}, u32[]{:S(2)}) %collective-permute-start.21) | collective-permute-done | bytes 69664 | tf_op jit(solution)/shard_map/ppermute | solution.py:20
  98.3 4.9 %collective-permute-start.24 = (f32[24,128]{1,0:T(8,128)S(1)}, f32[24,128]{1,0:T(8,128)S(1)}, u32[]{:S(2)}, u32[]{:S(2)}) collective-permute-start(f32[24,128]{1,0:T(8,128)S(1)} %get-tuple-element.108), channel_id=1, source_target_pairs={{0,64},{2,66},{4,68},{6,70},{8,72},{10,74},{12,76},{14,78},{16,80}... | collective-permute-start | bytes 36872 | tf_op jit(solution)/shard_map/ppermute | solution.py:20
  103.2 2.2 %collective-permute-start.26 = (f32[16,2176]{1,0:T(8,128)S(1)}, f32[16,2176]{1,0:T(8,128)S(1)}, u32[]{:S(2)}, u32[]{:S(2)}) collective-permute-start(f32[16,2176]{1,0:T(8,128)S(1)} %get-tuple-element.111), channel_id=1, source_target_pairs={{0,8},{2,10},{4,12},{6,14},{8,0},{10,2},{12,4},{14,6},{16,24},{18,... | collective-permute-start | bytes 417800 | tf_op jit(solution)/shard_map/ppermute | solution.py:20
  108.9 3.4 %collective-permute-done.26.refs_2_ = f32[16,2176]{1,0:T(8,128)S(1)} collective-permute-done((f32[16,2176]{1,0:T(8,128)S(1)}, f32[16,2176]{1,0:T(8,128)S(1)}, u32[]{:S(2)}, u32[]{:S(2)}) %collective-permute-start.26) | collective-permute-done | bytes 139296 | tf_op jit(solution)/shard_map/ppermute | solution.py:20
  114.6 9.7 %collective-permute-start.29 = (f32[16,2176]{1,0:T(8,128)S(1)}, f32[16,2176]{1,0:T(8,128)S(1)}, u32[]{:S(2)}, u32[]{:S(2)}) collective-permute-start(f32[16,2176]{1,0:T(8,128)S(1)} %get-tuple-element.118.give_ref), channel_id=1, source_target_pairs={{0,2},{2,0},{4,6},{6,4},{8,10},{10,8},{12,14},{14,12},{16,18},{18,... | collective-permute-start | bytes 417800 | tf_op jit(solution)/shard_map/ppermute | solution.py:20
  126.1 2.3 %collective-permute-done.28 = f32[24,128]{1,0:T(8,128)S(1)} collective-permute-done((f32[24,128]{1,0:T(8,128)S(1)}, f32[24,128]{1,0:T(8,128)S(1)}, u32[]{:S(2)}, u32[]{:S(2)}) %collective-permute-start.28) | collective-permute-done | bytes 12320 | tf_op jit(solution)/shard_map/ppermute | solution.py:20
  134.9 4.5 %collective-permute-done.34.refs_2_ = bf16[96,2048]{1,0:T(8,128)(2,1)S(1)} collective-permute-done((bf16[96,2048]{1,0:T(8,128)(2,1)S(1)}, bf16[96,2048]{1,0:T(8,128)(2,1)S(1)}, u32[]{:S(2)}, u32[]{:S(2)}) %collective-permute-start.34) | collective-permute-done | bytes 393248 | tf_op jit(solution)/shard_map/ppermute | solution.py:20
  140.5 2.2 %collective-permute-start.36 = (bf16[192,2048]{1,0:T(8,128)(2,1)S(1)}, bf16[192,2048]{1,0:T(8,128)(2,1)S(1)}, u32[]{:S(2)}, u32[]{:S(2)}) collective-permute-start(bf16[192,2048]{1,0:T(8,128)(2,1)S(1)} %shard_map.108), channel_id=1, source_target_pairs={{0,2},{2,0},{4,6},{6,4},{8,10},{10,8},{12,14},{14,12},{16,18},{18,... | collective-permute-start | bytes 2359304 | tf_op jit(solution)/shard_map/ppermute | solution.py:20
  142.8 2.6 %collective-permute-done.35 = f32[24,128]{1,0:T(8,128)S(1)} collective-permute-done((f32[24,128]{1,0:T(8,128)S(1)}, f32[24,128]{1,0:T(8,128)S(1)}, u32[]{:S(2)}, u32[]{:S(2)}) %collective-permute-start.35) | collective-permute-done | bytes 12320 | tf_op jit(solution)/shard_map/ppermute | solution.py:20
  146.2 6.9 %shard_map.109 = (bf16[512,2048]{1,0:T(8,128)(2,1)}, bf16[8,2048]{1,0:T(8,128)(2,1)}) custom-call(bf16[512,2048]{1,0:T(8,128)(2,1)} %hidden_ref.1, bf16[8,2048]{1,0:T(8,128)(2,1)} %passages.1, f32[1,2048]{1,0:T(1,128)} %bitcast.8, f32[2,640]{1,0:T(2,128)} %copy-done.12, f32[8,2048]{1,0:T(8,128)} %copy-done.8, f32[16,2176]{1,0:T(8,128)} %copy-done.7, ...), custom_call_target="tpu_custom_call" | custom-call | tf_op jit(solution)/shard_map/pallas_call | solution.py:405
  (128 shorter events, 51.4 us)
Async XLA Ops:
  4.5 7.5 %collective-permute-start = (bf16[8,2176]{1,0:T(8,128)(2,1)S(1)}, bf16[8,2176]{1,0:T(8,128)(2,1)S(1)}, u32[]{:S(2)}, u32[]{:S(2)}) collective-permute-start(bf16[8,2176]{1,0:T(8,128)(2,1)S(1)} %pad_maximum_fusion.4), channel_id=1, source_target_pairs={{0,128},{2,130},{4,132},{6,134},{8,136},{10,138},{12,140},{14,142}... | collective-permute-start | bytes 104456 | tf_op jit(solution)/shard_map/ppermute | solution.py:20
  8.3 24.0 %collective-permute-start.4 = (bf16[512,2048]{1,0:T(8,128)(2,1)}, bf16[512,2048]{1,0:T(8,128)(2,1)}, u32[]{:S(2)}, u32[]{:S(2)}) collective-permute-start(bf16[512,2048]{1,0:T(8,128)(2,1)} %hidden_ref.1), channel_id=1, source_target_pairs={{0,2},{2,0},{4,6},{6,4},{8,10},{10,8},{12,14},{14,12},{16,18},{18,... | collective-permute-start | bytes 6291464 | tf_op jit(solution)/shard_map/ppermute | solution.py:20
  12.0 9.7 %collective-permute-start.1 = (bf16[16,2176]{1,0:T(8,128)(2,1)S(1)}, bf16[16,2176]{1,0:T(8,128)(2,1)S(1)}, u32[]{:S(2)}, u32[]{:S(2)}) collective-permute-start(bf16[16,2176]{1,0:T(8,128)(2,1)S(1)} %pad_maximum_fusion.3), channel_id=1, source_target_pairs={{0,64},{2,66},{4,68},{6,70},{8,72},{10,74},{12,76},{14,78},{16,80}... | collective-permute-start | bytes 208904 | tf_op jit(solution)/shard_map/ppermute | solution.py:20
  21.9 11.7 %collective-permute-start.11 = (f32[1,512]{1,0:T(1,128)S(1)}, f32[1,512]{1,0:T(1,128)S(1)}, u32[]{:S(2)}, u32[]{:S(2)}) collective-permute-start(f32[1,512]{1,0:T(1,128)S(1)} %slice_divide_fusion), channel_id=1, source_target_pairs={{0,2},{2,0},{4,6},{6,4},{8,10},{10,8},{12,14},{14,12},{16,18},{18,... | collective-permute-start | bytes 6152 | tf_op jit(solution)/shard_map/ppermute | solution.py:20
  23.1 9.1 %collective-permute-start.3 = (bf16[32,2176]{1,0:T(8,128)(2,1)S(1)}, bf16[32,2176]{1,0:T(8,128)(2,1)S(1)}, u32[]{:S(2)}, u32[]{:S(2)}) collective-permute-start(bf16[32,2176]{1,0:T(8,128)(2,1)S(1)} %pad_maximum_fusion.2), channel_id=1, source_target_pairs={{0,32},{2,34},{4,36},{6,38},{8,40},{10,42},{12,44},{14,46},{16,48}... | collective-permute-start | bytes 417800 | tf_op jit(solution)/shard_map/ppermute | solution.py:20
  36.2 6.7 %collective-permute-start.5 = (bf16[64,2176]{1,0:T(8,128)(2,1)S(1)}, bf16[64,2176]{1,0:T(8,128)(2,1)S(1)}, u32[]{:S(2)}, u32[]{:S(2)}) collective-permute-start(bf16[64,2176]{1,0:T(8,128)(2,1)S(1)} %pad_maximum_fusion.1), channel_id=1, source_target_pairs={{0,16},{2,18},{4,20},{6,22},{8,24},{10,26},{12,28},{14,30},{16,0},... | collective-permute-start | bytes 835592 | tf_op jit(solution)/shard_map/ppermute | solution.py:20
  36.2 6.8 %collective-permute-start.10 = (bf16[8,2048]{1,0:T(8,128)(2,1)S(1)}, bf16[8,2048]{1,0:T(8,128)(2,1)S(1)}, u32[]{:S(2)}, u32[]{:S(2)}) collective-permute-start(bf16[8,2048]{1,0:T(8,128)(2,1)S(1)} %fusion.7.p_a), channel_id=1, source_target_pairs={{0,2},{2,0},{4,6},{6,4},{8,10},{10,8},{12,14},{14,12},{16,18},{18,... | collective-permute-start | bytes 98312 | tf_op jit(solution)/shard_map/ppermute | solution.py:20
  47.0 9.7 %collective-permute-start.12 = (bf16[112,2048]{1,0:T(8,128)(2,1)S(1)}, bf16[112,2048]{1,0:T(8,128)(2,1)S(1)}, u32[]{:S(2)}, u32[]{:S(2)}) collective-permute-start(bf16[112,2048]{1,0:T(8,128)(2,1)S(1)} %get-tuple-element.86), channel_id=1, source_target_pairs={{0,4},{2,6},{4,0},{6,2},{8,12},{10,14},{12,8},{14,10},{16,20},{18,... | collective-permute-start | bytes 1376264 | tf_op jit(solution)/shard_map/ppermute | solution.py:20
  47.5 20.2 %collective-permute-start.13 = (bf16[112,2048]{1,0:T(8,128)(2,1)S(1)}, bf16[112,2048]{1,0:T(8,128)(2,1)S(1)}, u32[]{:S(2)}, u32[]{:S(2)}) collective-permute-start(bf16[112,2048]{1,0:T(8,128)(2,1)S(1)} %get-tuple-element.87), channel_id=1, source_target_pairs={{0,8},{2,10},{4,12},{6,14},{8,0},{10,2},{12,4},{14,6},{16,24},{18,... | collective-permute-start | bytes 1376264 | tf_op jit(solution)/shard_map/ppermute | solution.py:20
  49.9 17.8 %collective-permute-start.14 = (bf16[112,2048]{1,0:T(8,128)(2,1)S(1)}, bf16[112,2048]{1,0:T(8,128)(2,1)S(1)}, u32[]{:S(2)}, u32[]{:S(2)}) collective-permute-start(bf16[112,2048]{1,0:T(8,128)(2,1)S(1)} %get-tuple-element.88), channel_id=1, source_target_pairs={{0,12},{2,14},{4,8},{6,10},{8,4},{10,6},{12,0},{14,2},{16,28},{18,... | collective-permute-start | bytes 1376264 | tf_op jit(solution)/shard_map/ppermute | solution.py:20
  72.9 11.4 %collective-permute-start.16 = (bf16[16,2176]{1,0:T(8,128)(2,1)S(1)}, bf16[16,2176]{1,0:T(8,128)(2,1)S(1)}, u32[]{:S(2)}, u32[]{:S(2)}) collective-permute-start(bf16[16,2176]{1,0:T(8,128)(2,1)S(1)} %get-tuple-element.92), channel_id=1, source_target_pairs={{0,64},{2,66},{4,68},{6,70},{8,72},{10,74},{12,76},{14,78},{16,80}... | collective-permute-start | bytes 208904 | tf_op jit(solution)/shard_map/ppermute | solution.py:20
  78.3 7.2 %collective-permute-start.17 = (bf16[16,2176]{1,0:T(8,128)(2,1)S(1)}, bf16[16,2176]{1,0:T(8,128)(2,1)S(1)}, u32[]{:S(2)}, u32[]{:S(2)}) collective-permute-start(bf16[16,2176]{1,0:T(8,128)(2,1)S(1)} %get-tuple-element.93), channel_id=1, source_target_pairs={{0,32},{2,34},{4,36},{6,38},{8,40},{10,42},{12,44},{14,46},{16,48}... | collective-permute-start | bytes 208904 | tf_op jit(solution)/shard_map/ppermute | solution.py:20
  79.0 6.9 %collective-permute-start.18 = (bf16[16,2176]{1,0:T(8,128)(2,1)S(1)}, bf16[16,2176]{1,0:T(8,128)(2,1)S(1)}, u32[]{:S(2)}, u32[]{:S(2)}) collective-permute-start(bf16[16,2176]{1,0:T(8,128)(2,1)S(1)} %get-tuple-element.94), channel_id=1, source_target_pairs={{0,96},{2,98},{4,100},{6,102},{8,104},{10,106},{12,108},{14,110},{... | collective-permute-start | bytes 208904 | tf_op jit(solution)/shard_map/ppermute | solution.py:20
  79.0 6.9 %collective-permute-start.19 = (bf16[16,2176]{1,0:T(8,128)(2,1)S(1)}, bf16[16,2176]{1,0:T(8,128)(2,1)S(1)}, u32[]{:S(2)}, u32[]{:S(2)}) collective-permute-start(bf16[16,2176]{1,0:T(8,128)(2,1)S(1)} %get-tuple-element.95), channel_id=1, source_target_pairs={{0,16},{2,18},{4,20},{6,22},{8,24},{10,26},{12,28},{14,30},{16,0},... | collective-permute-start | bytes 208904 | tf_op jit(solution)/shard_map/ppermute | solution.py:20
  79.9 6.3 %collective-permute-start.20 = (bf16[16,2176]{1,0:T(8,128)(2,1)S(1)}, bf16[16,2176]{1,0:T(8,128)(2,1)S(1)}, u32[]{:S(2)}, u32[]{:S(2)}) collective-permute-start(bf16[16,2176]{1,0:T(8,128)(2,1)S(1)} %get-tuple-element.96), channel_id=1, source_target_pairs={{0,80},{2,82},{4,84},{6,86},{8,88},{10,90},{12,92},{14,94},{16,64}... | collective-permute-start | bytes 208904 | tf_op jit(solution)/shard_map/ppermute | solution.py:20
  84.3 6.0 %collective-permute-start.21 = (bf16[16,2176]{1,0:T(8,128)(2,1)S(1)}, bf16[16,2176]{1,0:T(8,128)(2,1)S(1)}, u32[]{:S(2)}, u32[]{:S(2)}) collective-permute-start(bf16[16,2176]{1,0:T(8,128)(2,1)S(1)} %get-tuple-element.97), channel_id=1, source_target_pairs={{0,48},{2,50},{4,52},{6,54},{8,56},{10,58},{12,60},{14,62},{16,32}... | collective-permute-start | bytes 208904 | tf_op jit(solution)/shard_map/ppermute | solution.py:20
  93.0 35.4 %collective-permute-start.30 = (bf16[96,2048]{1,0:T(8,128)(2,1)S(1)}, bf16[96,2048]{1,0:T(8,128)(2,1)S(1)}, u32[]{:S(2)}, u32[]{:S(2)}) collective-permute-start(bf16[96,2048]{1,0:T(8,128)(2,1)S(1)} %get-tuple-element.120.refs_1_), channel_id=1, source_target_pairs={{0,4},{2,6},{4,0},{6,2},{8,12},{10,14},{12,8},{14,10},{16,20},{18,... | collective-permute-start | bytes 1179656 | tf_op jit(solution)/shard_map/ppermute | solution.py:20
  93.4 35.0 %collective-permute-start.31 = (bf16[96,2048]{1,0:T(8,128)(2,1)S(1)}, bf16[96,2048]{1,0:T(8,128)(2,1)S(1)}, u32[]{:S(2)}, u32[]{:S(2)}) collective-permute-start(bf16[96,2048]{1,0:T(8,128)(2,1)S(1)} %get-tuple-element.121.refs_3_), channel_id=1, source_target_pairs={{0,12},{2,14},{4,8},{6,10},{8,4},{10,6},{12,0},{14,2},{16,28},{18,... | collective-permute-start | bytes 1179656 | tf_op jit(solution)/shard_map/ppermute | solution.py:20
  98.3 7.0 %collective-permute-start.24 = (f32[24,128]{1,0:T(8,128)S(1)}, f32[24,128]{1,0:T(8,128)S(1)}, u32[]{:S(2)}, u32[]{:S(2)}) collective-permute-start(f32[24,128]{1,0:T(8,128)S(1)} %get-tuple-element.108), channel_id=1, source_target_pairs={{0,64},{2,66},{4,68},{6,70},{8,72},{10,74},{12,76},{14,78},{16,80}... | collective-permute-start | bytes 36872 | tf_op jit(solution)/shard_map/ppermute | solution.py:20
  103.2 9.0 %collective-permute-start.26 = (f32[16,2176]{1,0:T(8,128)S(1)}, f32[16,2176]{1,0:T(8,128)S(1)}, u32[]{:S(2)}, u32[]{:S(2)}) collective-permute-start(f32[16,2176]{1,0:T(8,128)S(1)} %get-tuple-element.111), channel_id=1, source_target_pairs={{0,8},{2,10},{4,12},{6,14},{8,0},{10,2},{12,4},{14,6},{16,24},{18,... | collective-permute-start | bytes 417800 | tf_op jit(solution)/shard_map/ppermute | solution.py:20
  105.4 8.5 %collective-permute-start.27 = (f32[16,2176]{1,0:T(8,128)S(1)}, f32[16,2176]{1,0:T(8,128)S(1)}, u32[]{:S(2)}, u32[]{:S(2)}) collective-permute-start(f32[16,2176]{1,0:T(8,128)S(1)} %get-tuple-element.112), channel_id=1, source_target_pairs={{0,12},{2,14},{4,8},{6,10},{8,4},{10,6},{12,0},{14,2},{16,28},{18,... | collective-permute-start | bytes 417800 | tf_op jit(solution)/shard_map/ppermute | solution.py:20
  114.6 13.8 %collective-permute-start.29 = (f32[16,2176]{1,0:T(8,128)S(1)}, f32[16,2176]{1,0:T(8,128)S(1)}, u32[]{:S(2)}, u32[]{:S(2)}) collective-permute-start(f32[16,2176]{1,0:T(8,128)S(1)} %get-tuple-element.118.give_ref), channel_id=1, source_target_pairs={{0,2},{2,0},{4,6},{6,4},{8,10},{10,8},{12,14},{14,12},{16,18},{18,... | collective-permute-start | bytes 417800 | tf_op jit(solution)/shard_map/ppermute | solution.py:20
  128.4 11.0 %collective-permute-start.34 = (bf16[96,2048]{1,0:T(8,128)(2,1)S(1)}, bf16[96,2048]{1,0:T(8,128)(2,1)S(1)}, u32[]{:S(2)}, u32[]{:S(2)}) collective-permute-start(bf16[96,2048]{1,0:T(8,128)(2,1)S(1)} %get-tuple-element.125.refs_2_), channel_id=1, source_target_pairs={{0,8},{2,10},{4,12},{6,14},{8,0},{10,2},{12,4},{14,6},{16,24},{18,... | collective-permute-start | bytes 1179656 | tf_op jit(solution)/shard_map/ppermute | solution.py:20
  145.3 7.8 %collective-permute-start.37 = (f32[24,128]{1,0:T(8,128)S(1)}, f32[24,128]{1,0:T(8,128)S(1)}, u32[]{:S(2)}, u32[]{:S(2)}) collective-permute-start(f32[24,128]{1,0:T(8,128)S(1)} %add.96), channel_id=1, source_target_pairs={{0,8},{2,10},{4,12},{6,14},{8,0},{10,2},{12,4},{14,6},{16,24},{18,... | collective-permute-start | bytes 36872 | tf_op jit(solution)/shard_map/ppermute | solution.py:20
  (28 other events, 370.7 us)

commit v3 on v2

--- a/solution.py
+++ b/solution.py
@@ -489,7 +489,8 @@
     )
     late = [late[0]] + [flip(late[s], 2 * s) for s in (1, 2, 3)]
     packed = packed + flip(packed, Z[2])
-    packed, *late = tie(packed, *late)
+    packed, second, *late = tie(packed, pair_q[2], *late)
+    second = flip(second, 4)
     own, give = call(
         late_kernel,
         jax.ShapeDtypeStruct((8, 2048), f32),
@@ -500,8 +501,7 @@
     )(slots, *late)
     got = flip(give, C)
     packed = packed + flip(packed, YH)
-    packed, got, first, third, second = tie(packed, got, first, third, pair_q[2])
-    second = flip(second, 4)
+    packed, got, first, third = tie(packed, got, first, third)
     for mask in (Z[1], Z[0]):
         packed = packed + flip(packed, mask)
     packed, second = tie(packed, second)

time: 159 us -> 160 us (level)
  starting transfers between devices: 69.5 us -> 79.5 us
  waiting for transfers between devices: 61 us -> 52.7 us
    ppermute x37, starting transfers between devices: 68.2 us -> 78.3 us  [flip(): return lax.ppermute(x, 'dp', [(i, i ^ mask) for i in range(128)])]
    ppermute x37, waiting for transfers between devices: 56.3 us -> 47.9 us  [flip(): return lax.ppermute(x, 'dp', [(i, i ^ mask) for i in range(128)])]
  transfers between devices with their start and end apart: 39 -> 39, of which waited for: 21 -> 18; matrix products, arithmetic and copies ran while one was open for 2% -> 2% of each run, Pallas kernels for 7% -> 5%
where the time goes in v3:
time: 160 us
  starting transfers between devices  79.5 us (50%)
  waiting for transfers between devices  52.7 us (33%)
  Pallas kernels  16.9 us (11%)
  other arithmetic  5.22 us (3%)
  between operations  2.82 us (2%)
  local copies, waits for them, and re-layouts  2.65 us (2%)
    ppermute x37, starting transfers between devices, flip(): return lax.ppermute(x, 'dp', [(i, i ^ mask) for i in range(128)])  78.3 us
    ppermute x37, waiting for transfers between devices, flip(): return lax.ppermute(x, 'dp', [(i, i ^ mask) for i in range(128)])  47.9 us
    pallas_call x9, Pallas kernels, run(): pl.pallas_call(kernel, out_shape=shapes, in_specs=[pl.BlockSpec(memory_sp...  16.9 us
  transfers between devices with their start and end apart: 39, of which 18 were waited for; matrix products, arithmetic and copies ran while one was open for 2% of the time, Pallas kernels for 5%

profile of v3, /device:TPU:1, one launch (start us, length us, event | category | flops | bytes accessed | tf_op | source)
XLA Modules:
  0.0 159.9 jit_solution(13044160802827406956)
XLA Ops:
  4.5 3.7 %collective-permute-start = (bf16[8,2176]{1,0:T(8,128)(2,1)S(1)}, bf16[8,2176]{1,0:T(8,128)(2,1)S(1)}, u32[]{:S(2)}, u32[]{:S(2)}) collective-permute-start(bf16[8,2176]{1,0:T(8,128)(2,1)S(1)} %pad_maximum_fusion.4), channel_id=1, source_target_pairs={{0,128},{2,130},{4,132},{6,134},{8,136},{10,138},{12,140},{14,142}... | collective-permute-start | bytes 104456 | tf_op jit(solution)/shard_map/ppermute | solution.py:20
  9.2 2.5 %fusion = (f32[512]{0:T(512)S(1)}, f32[512]{0:T(512)S(1)}) fusion(bf16[512,2048]{1,0:T(8,128)(2,1)} %hidden_ref.1, f32[2048]{0:T(1024)} %param.9), kind=kLoop, calls=%fused_computation.2 | loop fusion | flops 6290432 | bytes 2109440 | tf_op jit(solution)/shard_map/reduce_sum | solution.py:29
  12.0 7.0 %collective-permute-start.1 = (bf16[16,2176]{1,0:T(8,128)(2,1)S(1)}, bf16[16,2176]{1,0:T(8,128)(2,1)S(1)}, u32[]{:S(2)}, u32[]{:S(2)}) collective-permute-start(bf16[16,2176]{1,0:T(8,128)(2,1)S(1)} %pad_maximum_fusion.3), channel_id=1, source_target_pairs={{0,64},{2,66},{4,68},{6,70},{8,72},{10,74},{12,76},{14,78},{16,80}... | collective-permute-start | bytes 208904 | tf_op jit(solution)/shard_map/ppermute | solution.py:20
  19.4 2.3 %collective-permute-done.2 = f32[2,640]{1,0:T(2,128)S(1)} collective-permute-done((f32[2,640]{1,0:T(2,128)S(1)}, f32[2,640]{1,0:T(2,128)S(1)}, u32[]{:S(2)}, u32[]{:S(2)}) %collective-permute-start.2) | collective-permute-done | bytes 5152 | tf_op jit(solution)/shard_map/ppermute | solution.py:428
  23.1 2.3 %collective-permute-start.3 = (bf16[32,2176]{1,0:T(8,128)(2,1)S(1)}, bf16[32,2176]{1,0:T(8,128)(2,1)S(1)}, u32[]{:S(2)}, u32[]{:S(2)}) collective-permute-start(bf16[32,2176]{1,0:T(8,128)(2,1)S(1)} %pad_maximum_fusion.2), channel_id=1, source_target_pairs={{0,32},{2,34},{4,36},{6,38},{8,40},{10,42},{12,44},{14,46},{16,48}... | collective-permute-start | bytes 417800 | tf_op jit(solution)/shard_map/ppermute | solution.py:20
  25.5 6.7 %collective-permute-done.3 = bf16[32,2176]{1,0:T(8,128)(2,1)S(1)} collective-permute-done((bf16[32,2176]{1,0:T(8,128)(2,1)S(1)}, bf16[32,2176]{1,0:T(8,128)(2,1)S(1)}, u32[]{:S(2)}, u32[]{:S(2)}) %collective-permute-start.3) | collective-permute-done | bytes 139296 | tf_op jit(solution)/shard_map/ppermute | solution.py:20
  39.7 3.3 %collective-permute-done.5 = bf16[64,2176]{1,0:T(8,128)(2,1)S(1)} collective-permute-done((bf16[64,2176]{1,0:T(8,128)(2,1)S(1)}, bf16[64,2176]{1,0:T(8,128)(2,1)S(1)}, u32[]{:S(2)}, u32[]{:S(2)}) %collective-permute-start.5) | collective-permute-done | bytes 278560 | tf_op jit(solution)/shard_map/ppermute | solution.py:20
  44.0 2.9 %shard_map.102 = (bf16[112,2048]{1,0:T(8,128)(2,1)S(1)}, bf16[112,2048]{1,0:T(8,128)(2,1)S(1)}, bf16[112,2048]{1,0:T(8,128)(2,1)S(1)}, bf16[112,2048]{1,0:T(8,128)(2,1)S(1)}, s32[8,128]{1,0:T(8,128)S(1)}) custom-call(s32[1]{0:T(128)} %bitcast.2.me_ref, bf16[128,2176]{1,0:T(8,128)(2,1)S(1)} %pad_maximum_fusion.panel, bf16[512,2048]{1,0:T(8,128)(2,1)S(1)} %copy-done, ...), custom_call_target="tpu_custom_call" | custom-call | tf_op jit(solution)/shard_map/pallas_call | solution.py:405
  47.5 2.5 %collective-permute-start.13 = (bf16[112,2048]{1,0:T(8,128)(2,1)S(1)}, bf16[112,2048]{1,0:T(8,128)(2,1)S(1)}, u32[]{:S(2)}, u32[]{:S(2)}) collective-permute-start(bf16[112,2048]{1,0:T(8,128)(2,1)S(1)} %get-tuple-element.87), channel_id=1, source_target_pairs={{0,8},{2,10},{4,12},{6,14},{8,0},{10,2},{12,4},{14,6},{16,24},{18,... | collective-permute-start | bytes 1376264 | tf_op jit(solution)/shard_map/ppermute | solution.py:20
  51.9 4.8 %collective-permute-done.12.refs_5_.refs_1_ = bf16[112,2048]{1,0:T(8,128)(2,1)S(1)} collective-permute-done((bf16[112,2048]{1,0:T(8,128)(2,1)S(1)}, bf16[112,2048]{1,0:T(8,128)(2,1)S(1)}, u32[]{:S(2)}, u32[]{:S(2)}) %collective-permute-start.12) | collective-permute-done | bytes 458784 | tf_op jit(solution)/shard_map/ppermute | solution.py:20
  56.7 11.0 %collective-permute-done.13.refs_6_.refs_2_ = bf16[112,2048]{1,0:T(8,128)(2,1)S(1)} collective-permute-done((bf16[112,2048]{1,0:T(8,128)(2,1)S(1)}, bf16[112,2048]{1,0:T(8,128)(2,1)S(1)}, u32[]{:S(2)}, u32[]{:S(2)}) %collective-permute-start.13) | collective-permute-done | bytes 458784 | tf_op jit(solution)/shard_map/ppermute | solution.py:20
  69.5 2.4 %collective-permute-done.15.got = f32[72,128]{1,0:T(8,128)S(1)} collective-permute-done((f32[72,128]{1,0:T(8,128)S(1)}, f32[72,128]{1,0:T(8,128)S(1)}, u32[]{:S(2)}, u32[]{:S(2)}) %collective-permute-start.15) | collective-permute-done | bytes 36896 | tf_op jit(solution)/shard_map/ppermute | solution.py:456
  72.9 5.4 %collective-permute-start.16 = (bf16[16,2176]{1,0:T(8,128)(2,1)S(1)}, bf16[16,2176]{1,0:T(8,128)(2,1)S(1)}, u32[]{:S(2)}, u32[]{:S(2)}) collective-permute-start(bf16[16,2176]{1,0:T(8,128)(2,1)S(1)} %get-tuple-element.92), channel_id=1, source_target_pairs={{0,64},{2,66},{4,68},{6,70},{8,72},{10,74},{12,76},{14,78},{16,80}... | collective-permute-start | bytes 208904 | tf_op jit(solution)/shard_map/ppermute | solution.py:20
  79.9 4.4 %collective-permute-start.20 = (bf16[16,2176]{1,0:T(8,128)(2,1)S(1)}, bf16[16,2176]{1,0:T(8,128)(2,1)S(1)}, u32[]{:S(2)}, u32[]{:S(2)}) collective-permute-start(bf16[16,2176]{1,0:T(8,128)(2,1)S(1)} %get-tuple-element.96), channel_id=1, source_target_pairs={{0,80},{2,82},{4,84},{6,86},{8,88},{10,90},{12,92},{14,94},{16,64}... | collective-permute-start | bytes 208904 | tf_op jit(solution)/shard_map/ppermute | solution.py:20
  86.2 4.1 %collective-permute-done.21.refs_5_ = bf16[16,2176]{1,0:T(8,128)(2,1)S(1)} collective-permute-done((bf16[16,2176]{1,0:T(8,128)(2,1)S(1)}, bf16[16,2176]{1,0:T(8,128)(2,1)S(1)}, u32[]{:S(2)}, u32[]{:S(2)}) %collective-permute-start.21) | collective-permute-done | bytes 69664 | tf_op jit(solution)/shard_map/ppermute | solution.py:20
  93.0 3.3 %collective-permute-done.23.got = f32[16,2048]{1,0:T(8,128)S(1)} collective-permute-done((f32[16,2048]{1,0:T(8,128)S(1)}, f32[16,2048]{1,0:T(8,128)S(1)}, u32[]{:S(2)}, u32[]{:S(2)}) %collective-permute-start.23) | collective-permute-done | bytes 131104 | tf_op jit(solution)/shard_map/ppermute | solution.py:20
  96.3 2.1 %shard_map.106 = (f32[24,128]{1,0:T(8,128)S(1)}, f32[16,2176]{1,0:T(8,128)S(1)}, f32[16,2176]{1,0:T(8,128)S(1)}, f32[16,2176]{1,0:T(8,128)S(1)}, f32[16,2176]{1,0:T(8,128)S(1)}, /*index=5*/bf16[8,2048]{1,0:T(8,128)(2,1)}) custom-call(f32[8,2048]{1,0:T(8,128)S(1)} %get-tuple-element.102.kept, f32[16,2048]{1,0:T(8,128)S(1)} %collective-permute-done.23.got, ...), custom_call_target="tpu_custom_call" | custom-call | tf_op jit(solution)/shard_map/pallas_call | solution.py:405
  102.2 4.9 %collective-permute-start.24 = (f32[24,128]{1,0:T(8,128)S(1)}, f32[24,128]{1,0:T(8,128)S(1)}, u32[]{:S(2)}, u32[]{:S(2)}) collective-permute-start(f32[24,128]{1,0:T(8,128)S(1)} %get-tuple-element.108), channel_id=1, source_target_pairs={{0,64},{2,66},{4,68},{6,70},{8,72},{10,74},{12,76},{14,78},{16,80}... | collective-permute-start | bytes 36872 | tf_op jit(solution)/shard_map/ppermute | solution.py:20
  111.6 13.5 %collective-permute-start.29 = (f32[16,2176]{1,0:T(8,128)S(1)}, f32[16,2176]{1,0:T(8,128)S(1)}, u32[]{:S(2)}, u32[]{:S(2)}) collective-permute-start(f32[16,2176]{1,0:T(8,128)S(1)} %get-tuple-element.118.give_ref), channel_id=1, source_target_pairs={{0,2},{2,0},{4,6},{6,4},{8,10},{10,8},{12,14},{14,12},{16,18},{18,... | collective-permute-start | bytes 417800 | tf_op jit(solution)/shard_map/ppermute | solution.py:20
  127.0 2.5 %collective-permute-done.28 = f32[24,128]{1,0:T(8,128)S(1)} collective-permute-done((f32[24,128]{1,0:T(8,128)S(1)}, f32[24,128]{1,0:T(8,128)S(1)}, u32[]{:S(2)}, u32[]{:S(2)}) %collective-permute-start.28) | collective-permute-done | bytes 12320 | tf_op jit(solution)/shard_map/ppermute | solution.py:20
  131.0 2.3 %collective-permute-done.32 = f32[24,128]{1,0:T(8,128)S(1)} collective-permute-done((f32[24,128]{1,0:T(8,128)S(1)}, f32[24,128]{1,0:T(8,128)S(1)}, u32[]{:S(2)}, u32[]{:S(2)}) %collective-permute-start.32) | collective-permute-done | bytes 12320 | tf_op jit(solution)/shard_map/ppermute | solution.py:20
  137.0 7.4 %collective-permute-start.36 = (bf16[192,2048]{1,0:T(8,128)(2,1)S(1)}, bf16[192,2048]{1,0:T(8,128)(2,1)S(1)}, u32[]{:S(2)}, u32[]{:S(2)}) collective-permute-start(bf16[192,2048]{1,0:T(8,128)(2,1)S(1)} %shard_map.108), channel_id=1, source_target_pairs={{0,2},{2,0},{4,6},{6,4},{8,10},{10,8},{12,14},{14,12},{16,18},{18,... | collective-permute-start | bytes 2359304 | tf_op jit(solution)/shard_map/ppermute | solution.py:20
  144.5 2.6 %collective-permute-done.35 = f32[24,128]{1,0:T(8,128)S(1)} collective-permute-done((f32[24,128]{1,0:T(8,128)S(1)}, f32[24,128]{1,0:T(8,128)S(1)}, u32[]{:S(2)}, u32[]{:S(2)}) %collective-permute-start.35) | collective-permute-done | bytes 12320 | tf_op jit(solution)/shard_map/ppermute | solution.py:20
  147.9 6.9 %shard_map.109 = (bf16[512,2048]{1,0:T(8,128)(2,1)}, bf16[8,2048]{1,0:T(8,128)(2,1)}) custom-call(bf16[512,2048]{1,0:T(8,128)(2,1)} %hidden_ref.1, bf16[8,2048]{1,0:T(8,128)(2,1)} %passages.1, f32[1,2048]{1,0:T(1,128)} %bitcast.8, f32[2,640]{1,0:T(2,128)} %copy-done.12, f32[8,2048]{1,0:T(8,128)} %copy-done.8, f32[16,2176]{1,0:T(8,128)} %copy-done.7, ...), custom_call_target="tpu_custom_call" | custom-call | tf_op jit(solution)/shard_map/pallas_call | solution.py:405
  (128 shorter events, 46.2 us)
Async XLA Ops:
  4.5 7.5 %collective-permute-start = (bf16[8,2176]{1,0:T(8,128)(2,1)S(1)}, bf16[8,2176]{1,0:T(8,128)(2,1)S(1)}, u32[]{:S(2)}, u32[]{:S(2)}) collective-permute-start(bf16[8,2176]{1,0:T(8,128)(2,1)S(1)} %pad_maximum_fusion.4), channel_id=1, source_target_pairs={{0,128},{2,130},{4,132},{6,134},{8,136},{10,138},{12,140},{14,142}... | collective-permute-start | bytes 104456 | tf_op jit(solution)/shard_map/ppermute | solution.py:20
  8.3 24.0 %collective-permute-start.4 = (bf16[512,2048]{1,0:T(8,128)(2,1)}, bf16[512,2048]{1,0:T(8,128)(2,1)}, u32[]{:S(2)}, u32[]{:S(2)}) collective-permute-start(bf16[512,2048]{1,0:T(8,128)(2,1)} %hidden_ref.1), channel_id=1, source_target_pairs={{0,2},{2,0},{4,6},{6,4},{8,10},{10,8},{12,14},{14,12},{16,18},{18,... | collective-permute-start | bytes 6291464 | tf_op jit(solution)/shard_map/ppermute | solution.py:20
  12.0 9.7 %collective-permute-start.1 = (bf16[16,2176]{1,0:T(8,128)(2,1)S(1)}, bf16[16,2176]{1,0:T(8,128)(2,1)S(1)}, u32[]{:S(2)}, u32[]{:S(2)}) collective-permute-start(bf16[16,2176]{1,0:T(8,128)(2,1)S(1)} %pad_maximum_fusion.3), channel_id=1, source_target_pairs={{0,64},{2,66},{4,68},{6,70},{8,72},{10,74},{12,76},{14,78},{16,80}... | collective-permute-start | bytes 208904 | tf_op jit(solution)/shard_map/ppermute | solution.py:20
  21.9 11.7 %collective-permute-start.11 = (f32[1,512]{1,0:T(1,128)S(1)}, f32[1,512]{1,0:T(1,128)S(1)}, u32[]{:S(2)}, u32[]{:S(2)}) collective-permute-start(f32[1,512]{1,0:T(1,128)S(1)} %slice_divide_fusion), channel_id=1, source_target_pairs={{0,2},{2,0},{4,6},{6,4},{8,10},{10,8},{12,14},{14,12},{16,18},{18,... | collective-permute-start | bytes 6152 | tf_op jit(solution)/shard_map/ppermute | solution.py:20
  23.1 9.1 %collective-permute-start.3 = (bf16[32,2176]{1,0:T(8,128)(2,1)S(1)}, bf16[32,2176]{1,0:T(8,128)(2,1)S(1)}, u32[]{:S(2)}, u32[]{:S(2)}) collective-permute-start(bf16[32,2176]{1,0:T(8,128)(2,1)S(1)} %pad_maximum_fusion.2), channel_id=1, source_target_pairs={{0,32},{2,34},{4,36},{6,38},{8,40},{10,42},{12,44},{14,46},{16,48}... | collective-permute-start | bytes 417800 | tf_op jit(solution)/shard_map/ppermute | solution.py:20
  36.2 6.7 %collective-permute-start.5 = (bf16[64,2176]{1,0:T(8,128)(2,1)S(1)}, bf16[64,2176]{1,0:T(8,128)(2,1)S(1)}, u32[]{:S(2)}, u32[]{:S(2)}) collective-permute-start(bf16[64,2176]{1,0:T(8,128)(2,1)S(1)} %pad_maximum_fusion.1), channel_id=1, source_target_pairs={{0,16},{2,18},{4,20},{6,22},{8,24},{10,26},{12,28},{14,30},{16,0},... | collective-permute-start | bytes 835592 | tf_op jit(solution)/shard_map/ppermute | solution.py:20
  36.2 6.8 %collective-permute-start.10 = (bf16[8,2048]{1,0:T(8,128)(2,1)S(1)}, bf16[8,2048]{1,0:T(8,128)(2,1)S(1)}, u32[]{:S(2)}, u32[]{:S(2)}) collective-permute-start(bf16[8,2048]{1,0:T(8,128)(2,1)S(1)} %fusion.7.p_a), channel_id=1, source_target_pairs={{0,2},{2,0},{4,6},{6,4},{8,10},{10,8},{12,14},{14,12},{16,18},{18,... | collective-permute-start | bytes 98312 | tf_op jit(solution)/shard_map/ppermute | solution.py:20
  47.0 9.7 %collective-permute-start.12 = (bf16[112,2048]{1,0:T(8,128)(2,1)S(1)}, bf16[112,2048]{1,0:T(8,128)(2,1)S(1)}, u32[]{:S(2)}, u32[]{:S(2)}) collective-permute-start(bf16[112,2048]{1,0:T(8,128)(2,1)S(1)} %get-tuple-element.86), channel_id=1, source_target_pairs={{0,4},{2,6},{4,0},{6,2},{8,12},{10,14},{12,8},{14,10},{16,20},{18,... | collective-permute-start | bytes 1376264 | tf_op jit(solution)/shard_map/ppermute | solution.py:20
  47.5 20.2 %collective-permute-start.13 = (bf16[112,2048]{1,0:T(8,128)(2,1)S(1)}, bf16[112,2048]{1,0:T(8,128)(2,1)S(1)}, u32[]{:S(2)}, u32[]{:S(2)}) collective-permute-start(bf16[112,2048]{1,0:T(8,128)(2,1)S(1)} %get-tuple-element.87), channel_id=1, source_target_pairs={{0,8},{2,10},{4,12},{6,14},{8,0},{10,2},{12,4},{14,6},{16,24},{18,... | collective-permute-start | bytes 1376264 | tf_op jit(solution)/shard_map/ppermute | solution.py:20
  49.9 17.8 %collective-permute-start.14 = (bf16[112,2048]{1,0:T(8,128)(2,1)S(1)}, bf16[112,2048]{1,0:T(8,128)(2,1)S(1)}, u32[]{:S(2)}, u32[]{:S(2)}) collective-permute-start(bf16[112,2048]{1,0:T(8,128)(2,1)S(1)} %get-tuple-element.88), channel_id=1, source_target_pairs={{0,12},{2,14},{4,8},{6,10},{8,4},{10,6},{12,0},{14,2},{16,28},{18,... | collective-permute-start | bytes 1376264 | tf_op jit(solution)/shard_map/ppermute | solution.py:20
  72.9 11.4 %collective-permute-start.16 = (bf16[16,2176]{1,0:T(8,128)(2,1)S(1)}, bf16[16,2176]{1,0:T(8,128)(2,1)S(1)}, u32[]{:S(2)}, u32[]{:S(2)}) collective-permute-start(bf16[16,2176]{1,0:T(8,128)(2,1)S(1)} %get-tuple-element.92), channel_id=1, source_target_pairs={{0,64},{2,66},{4,68},{6,70},{8,72},{10,74},{12,76},{14,78},{16,80}... | collective-permute-start | bytes 208904 | tf_op jit(solution)/shard_map/ppermute | solution.py:20
  78.3 7.2 %collective-permute-start.17 = (bf16[16,2176]{1,0:T(8,128)(2,1)S(1)}, bf16[16,2176]{1,0:T(8,128)(2,1)S(1)}, u32[]{:S(2)}, u32[]{:S(2)}) collective-permute-start(bf16[16,2176]{1,0:T(8,128)(2,1)S(1)} %get-tuple-element.93), channel_id=1, source_target_pairs={{0,32},{2,34},{4,36},{6,38},{8,40},{10,42},{12,44},{14,46},{16,48}... | collective-permute-start | bytes 208904 | tf_op jit(solution)/shard_map/ppermute | solution.py:20
  79.0 6.9 %collective-permute-start.18 = (bf16[16,2176]{1,0:T(8,128)(2,1)S(1)}, bf16[16,2176]{1,0:T(8,128)(2,1)S(1)}, u32[]{:S(2)}, u32[]{:S(2)}) collective-permute-start(bf16[16,2176]{1,0:T(8,128)(2,1)S(1)} %get-tuple-element.94), channel_id=1, source_target_pairs={{0,96},{2,98},{4,100},{6,102},{8,104},{10,106},{12,108},{14,110},{... | collective-permute-start | bytes 208904 | tf_op jit(solution)/shard_map/ppermute | solution.py:20
  79.0 6.9 %collective-permute-start.19 = (bf16[16,2176]{1,0:T(8,128)(2,1)S(1)}, bf16[16,2176]{1,0:T(8,128)(2,1)S(1)}, u32[]{:S(2)}, u32[]{:S(2)}) collective-permute-start(bf16[16,2176]{1,0:T(8,128)(2,1)S(1)} %get-tuple-element.95), channel_id=1, source_target_pairs={{0,16},{2,18},{4,20},{6,22},{8,24},{10,26},{12,28},{14,30},{16,0},... | collective-permute-start | bytes 208904 | tf_op jit(solution)/shard_map/ppermute | solution.py:20
  98.3 11.8 %collective-permute-start.25 = (f32[16,2176]{1,0:T(8,128)S(1)}, f32[16,2176]{1,0:T(8,128)S(1)}, u32[]{:S(2)}, u32[]{:S(2)}) collective-permute-start(f32[16,2176]{1,0:T(8,128)S(1)} %get-tuple-element.110), channel_id=1, source_target_pairs={{0,4},{2,6},{4,0},{6,2},{8,12},{10,14},{12,8},{14,10},{16,20},{18,... | collective-permute-start | bytes 417800 | tf_op jit(solution)/shard_map/ppermute | solution.py:20
  99.6 10.5 %collective-permute-start.26 = (f32[16,2176]{1,0:T(8,128)S(1)}, f32[16,2176]{1,0:T(8,128)S(1)}, u32[]{:S(2)}, u32[]{:S(2)}) collective-permute-start(f32[16,2176]{1,0:T(8,128)S(1)} %get-tuple-element.111), channel_id=1, source_target_pairs={{0,8},{2,10},{4,12},{6,14},{8,0},{10,2},{12,4},{14,6},{16,24},{18,... | collective-permute-start | bytes 417800 | tf_op jit(solution)/shard_map/ppermute | solution.py:20
  100.9 9.2 %collective-permute-start.27 = (f32[16,2176]{1,0:T(8,128)S(1)}, f32[16,2176]{1,0:T(8,128)S(1)}, u32[]{:S(2)}, u32[]{:S(2)}) collective-permute-start(f32[16,2176]{1,0:T(8,128)S(1)} %get-tuple-element.112), channel_id=1, source_target_pairs={{0,12},{2,14},{4,8},{6,10},{8,4},{10,6},{12,0},{14,2},{16,28},{18,... | collective-permute-start | bytes 417800 | tf_op jit(solution)/shard_map/ppermute | solution.py:20
  102.2 6.5 %collective-permute-start.24 = (f32[24,128]{1,0:T(8,128)S(1)}, f32[24,128]{1,0:T(8,128)S(1)}, u32[]{:S(2)}, u32[]{:S(2)}) collective-permute-start(f32[24,128]{1,0:T(8,128)S(1)} %get-tuple-element.108), channel_id=1, source_target_pairs={{0,64},{2,66},{4,68},{6,70},{8,72},{10,74},{12,76},{14,78},{16,80}... | collective-permute-start | bytes 36872 | tf_op jit(solution)/shard_map/ppermute | solution.py:20
  107.1 22.4 %collective-permute-start.30 = (bf16[96,2048]{1,0:T(8,128)(2,1)S(1)}, bf16[96,2048]{1,0:T(8,128)(2,1)S(1)}, u32[]{:S(2)}, u32[]{:S(2)}) collective-permute-start(bf16[96,2048]{1,0:T(8,128)(2,1)S(1)} %get-tuple-element.120.refs_1_), channel_id=1, source_target_pairs={{0,4},{2,6},{4,0},{6,2},{8,12},{10,14},{12,8},{14,10},{16,20},{18,... | collective-permute-start | bytes 1179656 | tf_op jit(solution)/shard_map/ppermute | solution.py:20
  108.7 20.8 %collective-permute-start.31 = (bf16[96,2048]{1,0:T(8,128)(2,1)S(1)}, bf16[96,2048]{1,0:T(8,128)(2,1)S(1)}, u32[]{:S(2)}, u32[]{:S(2)}) collective-permute-start(bf16[96,2048]{1,0:T(8,128)(2,1)S(1)} %get-tuple-element.121.refs_3_), channel_id=1, source_target_pairs={{0,12},{2,14},{4,8},{6,10},{8,4},{10,6},{12,0},{14,2},{16,28},{18,... | collective-permute-start | bytes 1179656 | tf_op jit(solution)/shard_map/ppermute | solution.py:20
  110.1 25.8 %collective-permute-start.34 = (bf16[96,2048]{1,0:T(8,128)(2,1)S(1)}, bf16[96,2048]{1,0:T(8,128)(2,1)S(1)}, u32[]{:S(2)}, u32[]{:S(2)}) collective-permute-start(bf16[96,2048]{1,0:T(8,128)(2,1)S(1)} %get-tuple-element.125.refs_2_), channel_id=1, source_target_pairs={{0,8},{2,10},{4,12},{6,14},{8,0},{10,2},{12,4},{14,6},{16,24},{18,... | collective-permute-start | bytes 1179656 | tf_op jit(solution)/shard_map/ppermute | solution.py:20
  111.6 17.9 %collective-permute-start.29 = (f32[16,2176]{1,0:T(8,128)S(1)}, f32[16,2176]{1,0:T(8,128)S(1)}, u32[]{:S(2)}, u32[]{:S(2)}) collective-permute-start(f32[16,2176]{1,0:T(8,128)S(1)} %get-tuple-element.118.give_ref), channel_id=1, source_target_pairs={{0,2},{2,0},{4,6},{6,4},{8,10},{10,8},{12,14},{14,12},{16,18},{18,... | collective-permute-start | bytes 417800 | tf_op jit(solution)/shard_map/ppermute | solution.py:20
  137.0 10.0 %collective-permute-start.36 = (bf16[192,2048]{1,0:T(8,128)(2,1)S(1)}, bf16[192,2048]{1,0:T(8,128)(2,1)S(1)}, u32[]{:S(2)}, u32[]{:S(2)}) collective-permute-start(bf16[192,2048]{1,0:T(8,128)(2,1)S(1)} %shard_map.108), channel_id=1, source_target_pairs={{0,2},{2,0},{4,6},{6,4},{8,10},{10,8},{12,14},{14,12},{16,18},{18,... | collective-permute-start | bytes 2359304 | tf_op jit(solution)/shard_map/ppermute | solution.py:20
  147.1 7.8 %collective-permute-start.37 = (f32[24,128]{1,0:T(8,128)S(1)}, f32[24,128]{1,0:T(8,128)S(1)}, u32[]{:S(2)}, u32[]{:S(2)}) collective-permute-start(f32[24,128]{1,0:T(8,128)S(1)} %add.96), channel_id=1, source_target_pairs={{0,8},{2,10},{4,12},{6,14},{8,0},{10,2},{12,4},{14,6},{16,24},{18,... | collective-permute-start | bytes 36872 | tf_op jit(solution)/shard_map/ppermute | solution.py:20
  (28 other events, 386.0 us)
